TPU v7x, 32 devices: a whole 2x2x4 slice. The times are simulated.
32 devices in a mesh: expert: 4 (over y, x), shard: 8 (over z, core).
Axes of the slice: x: 2, y: 2, z: 4, core: 2. Of those that a mesh axis runs over, the one named last changes fastest.
Arguments:
- inputs: bfloat16 [16384, 1536], P(('expert', 'shard')), may hold values from -6 to 6
- attn_gain: bfloat16 [1536], P('shard'), may hold values from 0.5 to 1.5
- qkv_weight: bfloat16 [1536, 2560], P('shard'), may hold values from -0.21875 to 0.21875
- out_weight: bfloat16 [1536, 1536], P('shard'), may hold values from -0.4375 to 0.4375
- ffn_gain: bfloat16 [1536], P('shard'), may hold values from 0.5 to 1.5
- router_weight: bfloat16 [1536, 20], P('shard'), may hold values from -0.078125 to 0.078125
- expand_weight: bfloat16 [20, 1536, 1024], P('expert', 'shard'), may hold values from -0.15625 to 0.15625
- project_weight: bfloat16 [20, 512, 1536], P('expert', 'shard'), may hold values from -1.5 to 1.5
- segment_ids: int32 [32, 512], P(('expert', 'shard')), may hold values from 0 to 3, never falling along the last dimension, each value on 1 to 256 neighbouring positions
- routes: int32 [16384, 8], P(('expert', 'shard')), may hold values from 0 to 19, all different within a row; in each aligned block of 512 rows (0 to 511, 512 to 1023, ...) at most 256 rows name the same one
- out_grad: bfloat16 [16384, 1536], P(('expert', 'shard')), may hold values from -6 to 6
Outputs:
- output: bfloat16 [16384, 1536], P(('expert', 'shard'))
- input_grad: float32 [16384, 1536], P(('expert', 'shard'))
- attn_gain_grad: float32 [1536], P('shard')
- qkv_grad: float32 [1536, 2560], P('shard')
- out_weight_grad: float32 [1536, 1536], P('shard')
- ffn_gain_grad: float32 [1536], P('shard')
- router_grad: float32 [1536, 20], P('shard')
- expand_grad: float32 [20, 1536, 1024], P('expert', 'shard')
- project_grad: float32 [20, 512, 1536], P('expert', 'shard')
Inputs may be any that keep to these rules, and one draw needn't show every extreme that they name: `routes`: each row names 8 different experts. Within the 512 rows of one device no expert is named by more than 256 rows, and in every draw some expert is named by exactly 256 rows of some device. `segment_ids`: along each sequence the numbers never fall; each document holds 1 to 256 places and one holds exactly 256.
All inputs are finite; a program needn't handle non-finite values.
Results may differ from a plain program's by a relative error of at most 0.023.
Values may be sent and summed in bfloat16 or wider, within the bound.
A program may use at most 320 MiB of HBM per device.

v0:
```python
import functools

import jax
import jax.numpy as jnp
import numpy as np
from jax import lax
from jax.experimental import pallas as pl
from jax.experimental.pallas import tpu as pltpu
from jax.sharding import PartitionSpec as P

HEADS = 24
KV_HEADS = 8
HEAD = 64
FF = 512
TOP = 8
SEQ_LEN = 512
GROUP = HEADS // KV_HEADS
PAIRS = KV_HEADS // 2
QW = 2 * GROUP * HEAD
KW = 2 * HEAD
BLOCK = QW + 2 * KW
MISC = 128
QB = 128

EPSILON = 1e-06
ROPE_THETA = 10000.0
MASKED = -1e30
F32 = jnp.float32
BF16 = jnp.bfloat16


def dot_nn(a, b):
    return lax.dot_general(a, b, (((1,), (0,)), ((), ())), preferred_element_type=F32)


def dot_nt(a, b):
    return lax.dot_general(a, b, (((1,), (1,)), ((), ())), preferred_element_type=F32)


def dot_tn(a, b):
    return lax.dot_general(a, b, (((0,), (0,)), ((), ())), preferred_element_type=F32)


def rope_tables():
    frequency = (np.float32(ROPE_THETA) ** (-2.0 * np.arange(HEAD // 2) / HEAD)).astype(np.float32)
    angle = np.arange(SEQ_LEN, dtype=np.float32)[:, None] * frequency[None, :]
    cosine, sine = np.cos(angle).astype(np.float32), np.sin(angle).astype(np.float32)
    zero = np.zeros_like(sine)
    cos_table = np.concatenate([cosine] * 4, axis=1)
    left_table = np.concatenate([-sine, zero] * 2, axis=1)
    right_table = np.concatenate([zero, sine] * 2, axis=1)
    return cos_table, left_table, right_table


def turn(values, cos_table, left_table, right_table, sign):
    parts = []
    for c in range(values.shape[1] // 128):
        piece = values[:, 128 * c : 128 * (c + 1)]
        ahead = pltpu.roll(piece, 96, 1) * left_table
        behind = pltpu.roll(piece, 32, 1) * right_table
        parts.append(piece * cos_table + sign * (ahead + behind))
    return parts[0] if len(parts) == 1 else jnp.concatenate(parts, axis=1)


def key_range(block):
    return max(0, block - 2) * QB, (block + 1) * QB


def block_mask(seg_col, seg_row, block):
    low, high = key_range(block)
    rows = lax.broadcasted_iota(jnp.int32, (QB, high - low), 0) + block * QB
    cols = lax.broadcasted_iota(jnp.int32, (QB, high - low), 1) + low
    same = seg_col[block * QB : (block + 1) * QB, :] == seg_row[:, low:high]
    return jnp.concatenate([(rows >= cols) & same] * GROUP, axis=0)


def heads_of(values, pair, block):
    rows = values[block * QB : (block + 1) * QB, :]
    first = pair * GROUP
    return jnp.concatenate(
        [rows[:, HEAD * h : HEAD * (h + 1)] for h in range(first, first + GROUP)], axis=0
    )


def attention_forward_kernel(
    parts, levels, x_ref, gain_ref, w_ref, cos_ref, left_ref, right_ref, seg_col_ref, seg_row_ref,
    part_ref, normed_t_ref, proj_ref, mixed_ref, lse_ref, full_ref, normed_ref, *sems,
):
    step = pl.program_id(0)
    plan = Gather(parts, levels, [full_ref], sems)

    @pl.when(step == 0)
    def _():
        plan.greet(near=False)
        plan.own_to_mate(lambda: full_ref.at[pl.ds(plan.shard * parts, parts)], 0)
        for k in range(1, levels):
            plan.spread(0, k)

    @pl.when(step == 0)
    def _():
        x = x_ref[...].astype(F32)
        scale = lax.rsqrt(jnp.mean(x * x, axis=-1, keepdims=True) + EPSILON)
        normed = (x * scale * gain_ref[...].astype(F32)).astype(BF16)
        normed_ref[...] = normed
        normed_t_ref[...] = normed.T

    projected = dot_nn(normed_ref[...], w_ref[...])
    turned = turn(projected[:, : QW + KW], cos_ref[...], left_ref[...], right_ref[...], 1.0)
    queries = (turned[:, :QW] * HEAD**-0.5).astype(BF16)
    keys = turned[:, QW:].astype(BF16)
    values = projected[:, QW + KW :].astype(BF16)
    proj_ref[...] = jnp.concatenate([queries, keys, values], axis=1)
    seg_col, seg_row = seg_col_ref[...], seg_row_ref[...]
    for block in range(SEQ_LEN // QB):
        low, high = key_range(block)
        allowed = block_mask(seg_col, seg_row, block)
        outs = []
        for pair in range(2):
            q3 = heads_of(queries, pair, block)
            k1 = keys[low:high, HEAD * pair : HEAD * (pair + 1)]
            v1 = values[low:high, HEAD * pair : HEAD * (pair + 1)]
            scores = jnp.where(allowed, dot_nt(q3, k1), MASKED)
            top = jnp.max(scores, axis=-1, keepdims=True)
            weights = jnp.exp(scores - top)
            total = jnp.sum(weights, axis=-1, keepdims=True)
            mixed = dot_nn(weights.astype(BF16), v1) * (1.0 / total)
            logsum = top + jnp.log(total)
            for h in range(GROUP):
                outs.append(mixed[h * QB : (h + 1) * QB, :])
                lse_ref[0, block * QB : (block + 1) * QB, pair * GROUP + h : pair * GROUP + h + 1] = (
                    logsum[h * QB : (h + 1) * QB, :]
                )
        mixed_ref[block * QB : (block + 1) * QB, :] = jnp.concatenate(outs, axis=1).astype(BF16)

    @pl.when(step == PAIRS - 1)
    def _():
        plan.team_to_mate(0)
        plan.mate_arrived(0)
        plan.finish()


def whole_spec(shape):
    return pl.BlockSpec(shape, lambda *_: (0,) * len(shape))


def attention_forward(x, gain_row, w_full, tables, seg_col, seg_row, out_part, groups, shards):
    tokens, width = x.shape
    parts, levels = gather_parts(groups, width // shards), shards // 2
    table = whole_spec((SEQ_LEN, 128))
    *kept, out_full = pl.pallas_call(
        functools.partial(attention_forward_kernel, parts, levels),
        grid=(PAIRS,),
        in_specs=[
            whole_spec((tokens, width)),
            whole_spec((1, width)),
            pl.BlockSpec((width, BLOCK), lambda j: (0, j)),
            table, table, table,
            whole_spec((SEQ_LEN, 1)),
            whole_spec((1, SEQ_LEN)),
            pl.BlockSpec(memory_space=pl.ANY),
        ],
        out_specs=[
            whole_spec((width, tokens)),
            pl.BlockSpec((tokens, BLOCK), lambda j: (0, j)),
            pl.BlockSpec((tokens, QW), lambda j: (0, j)),
            pl.BlockSpec((1, tokens, 8), lambda j: (j, 0, 0)),
            pl.BlockSpec(memory_space=pl.ANY),
        ],
        out_shape=[
            jax.ShapeDtypeStruct((width, tokens), BF16),
            jax.ShapeDtypeStruct((tokens, PAIRS * BLOCK), BF16),
            jax.ShapeDtypeStruct((tokens, HEADS * HEAD), BF16),
            jax.ShapeDtypeStruct((PAIRS, tokens, 8), F32),
            jax.ShapeDtypeStruct(out_part.shape, BF16),
        ],
        scratch_shapes=[pltpu.VMEM((tokens, width), BF16)] + gather_sems(levels, parts, 1),
        input_output_aliases={8: 4},
        compiler_params=pltpu.CompilerParams(
            vmem_limit_bytes=62 << 20, collective_id=4, has_side_effects=True
        ),
        cost_estimate=pl.CostEstimate(flops=10 * 10**9, bytes_accessed=20 << 20, transcendentals=4 << 20),
        name="attention_forward",
    )(x, gain_row, w_full, *tables, seg_col, seg_row, out_part)
    return *kept, out_full.reshape(width, -1)


def attention_backward_kernel(
    groups, levels, ag_ref, out_ref, proj_ref, mixed_ref, lse_ref, cos_ref, left_ref, right_ref,
    seg_col_ref, seg_row_ref, all_ref, dproj_ref, sum_ref, mixed_t, *rest,
):
    step = pl.program_id(0)
    plan = Reduce(groups, levels, ag_ref.shape[1], rest[:4], rest[4:])

    @pl.when(step == 0)
    def _():
        plan.greet(False)
        mixed_t[...] = all_ref[...].T
        plan.fill(mixed_t, ag_ref)
        plan.merge()

    @pl.when(step == 1)
    def _():
        plan.spread()

    grads = dot_nt(ag_ref[...], out_ref[...]).astype(BF16)
    product = grads.astype(F32) * mixed_ref[...].astype(F32)
    queries, keys, values = (
        proj_ref[:, :QW], proj_ref[:, QW : QW + KW], proj_ref[:, QW + KW :],
    )
    seg_col, seg_row = seg_col_ref[...], seg_row_ref[...]
    blocks = SEQ_LEN // QB
    dk = [[jnp.zeros((QB, HEAD), F32) for _ in range(blocks)] for _ in range(2)]
    dv = [[jnp.zeros((QB, HEAD), F32) for _ in range(blocks)] for _ in range(2)]
    dq_rows = []
    for block in range(blocks):
        low, high = key_range(block)
        allowed = block_mask(seg_col, seg_row, block)
        dqs = []
        for pair in range(2):
            q3, g3, o3 = (heads_of(v, pair, block) for v in (queries, grads, product))
            k1 = keys[low:high, HEAD * pair : HEAD * (pair + 1)]
            v1 = values[low:high, HEAD * pair : HEAD * (pair + 1)]
            logsum = jnp.concatenate(
                [
                    lse_ref[0, block * QB : (block + 1) * QB, pair * GROUP + h : pair * GROUP + h + 1]
                    for h in range(GROUP)
                ],
                axis=0,
            )
            scores = jnp.where(allowed, dot_nt(q3, k1), MASKED)
            probs = jnp.exp(scores - logsum)
            inner = jnp.sum(o3, axis=-1, keepdims=True)
            score_grads = (probs * (dot_nt(g3, v1) - inner)).astype(BF16)
            dq = dot_nn(score_grads, k1)
            dk_part = dot_tn(score_grads, q3)
            dv_part = dot_tn(probs.astype(BF16), g3)
            for at in range(low // QB, high // QB):
                rows = slice(at * QB - low, (at + 1) * QB - low)
                dk[pair][at] += dk_part[rows]
                dv[pair][at] += dv_part[rows]
            dqs += [dq[h * QB : (h + 1) * QB, :] for h in range(GROUP)]
        dq_rows.append(jnp.concatenate(dqs, axis=1))
    dq_all = jnp.concatenate(dq_rows, axis=0)
    dk_all = jnp.concatenate([jnp.concatenate(d, axis=0) for d in dk], axis=1)
    dv_all = jnp.concatenate([jnp.concatenate(d, axis=0) for d in dv], axis=1)
    turned = jnp.concatenate([dq_all * HEAD**-0.5, dk_all], axis=1)
    back = turn(turned, cos_ref[...], left_ref[...], right_ref[...], -1.0)
    dproj_ref[...] = jnp.concatenate([back, dv_all], axis=1).astype(BF16)

    @pl.when(step == PAIRS - 1)
    def _():
        for k in range(levels):
            sum_ref[k] = plan.collect(k).astype(BF16)
        plan.finish()


def attention_backward(ag, out_full, proj, mixed, lse, tables, seg_col, seg_row, groups, shards):
    tokens, width = ag.shape
    levels, rows = shards // 2, width // shards
    chunk = chunk_of(width, groups)
    table = whole_spec((SEQ_LEN, 128))
    return pl.pallas_call(
        functools.partial(attention_backward_kernel, groups, levels),
        grid=(PAIRS,),
        in_specs=[
            whole_spec((tokens, width)),
            pl.BlockSpec((QW, width), lambda j: (j, 0)),
            pl.BlockSpec((tokens, BLOCK), lambda j: (0, j)),
            pl.BlockSpec((tokens, QW), lambda j: (0, j)),
            pl.BlockSpec((1, tokens, 8), lambda j: (j, 0, 0)),
            table, table, table,
            whole_spec((SEQ_LEN, 1)),
            whole_spec((1, SEQ_LEN)),
            whole_spec((tokens, mixed.shape[1])),
        ],
        out_specs=[
            pl.BlockSpec((tokens, BLOCK), lambda j: (0, j)),
            whole_spec((levels, rows, chunk)),
        ],
        out_shape=[
            jax.ShapeDtypeStruct((tokens, PAIRS * BLOCK), BF16),
            jax.ShapeDtypeStruct((levels, rows, chunk), BF16),
        ],
        scratch_shapes=[pltpu.VMEM((mixed.shape[1], tokens), BF16)]
        + reduce_buffers(groups, levels, rows, chunk)
        + reduce_sems(groups, levels),
        compiler_params=pltpu.CompilerParams(
            vmem_limit_bytes=62 << 20, collective_id=5, has_side_effects=True
        ),
        cost_estimate=pl.CostEstimate(flops=10 * 10**9, bytes_accessed=20 << 20, transcendentals=4 << 20),
        name="attention_backward",
    )(ag, out_full, proj, mixed, lse, *tables, seg_col, seg_row, mixed)


def middle_kernel(
    mixed_ref, out_ref, x_ref, gain_ref, router_ref, routes_ref,
    hidden_ref, ffn_ref, gates_ref, meta_ref,
):
    hidden = x_ref[...].astype(F32) + dot_nn(mixed_ref[...], out_ref[...])
    scale = lax.rsqrt(jnp.mean(hidden * hidden, axis=-1, keepdims=True) + EPSILON)
    hidden_ref[...] = hidden
    ffn_in = (hidden * scale * gain_ref[...].astype(F32)).astype(BF16)
    ffn_ref[...] = ffn_in
    logits = dot_nt(router_ref[...], ffn_in)
    experts, tokens = logits.shape
    index = lax.broadcasted_iota(jnp.int32, (experts, tokens), 0)
    flags = index == routes_ref[0:1, :]
    for k in range(1, TOP):
        flags = flags | (index == routes_ref[k : k + 1, :])
    chosen = jnp.where(flags, logits, MASKED)
    weights = jnp.where(flags, jnp.exp(chosen - jnp.max(chosen, axis=0, keepdims=True)), 0.0)
    gates = weights / jnp.sum(weights, axis=0, keepdims=True)
    gates_ref[...] = gates
    earlier = lax.broadcasted_iota(jnp.int32, (tokens, tokens), 0)
    later = lax.broadcasted_iota(jnp.int32, (tokens, tokens), 1)
    before = jnp.where(earlier < later, 1.0, 0.0).astype(BF16)
    ranks = dot_nn(jnp.where(flags, 1.0, 0.0).astype(BF16), before)
    slots = jnp.where(flags, ranks, -1.0)
    groups = meta_ref.shape[0]
    count = experts // groups
    meta_ref[...] = jnp.zeros(meta_ref.shape, F32)
    for e in range(experts):
        meta_ref[e // count, e % count : e % count + 1, :] = slots[e : e + 1]
        meta_ref[e // count, 8 + e % count : 9 + e % count, :] = gates[e : e + 1]


def middle(mixed, out_full, x, gain_row, router_rows, routes_rows, groups):
    tokens, width = x.shape
    experts = router_rows.shape[0]
    return pl.pallas_call(
        middle_kernel,
        out_shape=[
            jax.ShapeDtypeStruct((tokens, width), F32),
            jax.ShapeDtypeStruct((tokens, width), BF16),
            jax.ShapeDtypeStruct((experts, tokens), F32),
            jax.ShapeDtypeStruct((groups, 16, tokens), F32),
        ],
        compiler_params=pltpu.CompilerParams(vmem_limit_bytes=62 << 20),
        cost_estimate=pl.CostEstimate(flops=3 * 10**9, bytes_accessed=16 << 20, transcendentals=1 << 14),
        name="middle",
    )(mixed, out_full, x, gain_row, router_rows, routes_rows)


def flipped(index, mask):
    out, bit = index, 1
    while bit <= mask:
        if mask & bit:
            out = out + bit - 2 * bit * ((index // bit) % 2)
        bit *= 2
    return out


def send(source, target, send_sem, recv_sem, device):
    return pltpu.make_async_remote_copy(
        src_ref=source, dst_ref=target, send_sem=send_sem, recv_sem=recv_sem,
        device_id=device, device_id_type=pl.DeviceIdType.MESH,
    )


def greet(devices):
    barrier = pltpu.get_barrier_semaphore()
    for device in devices:
        pl.semaphore_signal(barrier, inc=1, device_id=device, device_id_type=pl.DeviceIdType.MESH)
    pl.semaphore_wait(barrier, len(devices))


class Gather:
    def __init__(self, parts, levels, blocks, sems):
        self.parts, self.levels, self.blocks = parts, levels, blocks
        self.near_send, self.near_recv, self.team_send, self.team_recv, self.core_send, self.core_recv = sems
        self.group, self.shard = lax.axis_index("expert"), lax.axis_index("shard")
        level, self.core = self.shard // 2, self.shard % 2
        self.part = self.group % parts
        self.other = self.shard + 1 - 2 * self.core
        self.far = [flipped(level, k) * 2 + self.core for k in range(levels)]
        self.far_other = [flipped(level, k) * 2 + 1 - self.core for k in range(levels)]
        self.team_part = [flipped(self.part, k) for k in range(parts)]
        self.team = [self.group - self.part + t for t in self.team_part]
        self.mate = (self.group, self.other)
        self.sends = []

    def greet(self, near=True):
        greet(
            [self.mate]
            + [(self.group, self.far[k]) for k in range(1, self.levels) if near]
            + [(self.team[t], self.shard) for t in range(1, self.parts)]
        )

    def push(self, make):
        make().start()
        self.sends.append(make)

    def arrived(self, piece, send_sem, recv_sem):
        send(piece, piece, send_sem, recv_sem, self.mate).wait_recv()

    def near(self, own, i):
        for k in range(1, self.levels):
            self.push(
                lambda k=k: send(
                    own.at[self.part], self.blocks[i].at[self.shard * self.parts + self.part],
                    self.near_send.at[i, k], self.near_recv.at[i, k], (self.group, self.far[k]),
                )
            )

    def near_arrived(self, i, k):
        piece = self.blocks[i].at[self.far[k] * self.parts + self.part]
        self.arrived(piece, self.near_send.at[i, k], self.near_recv.at[i, k])

    def spread(self, i, k):
        def piece():
            return self.blocks[i].at[self.far[k] * self.parts + self.part]

        for t in range(1, self.parts):
            self.push(
                lambda t=t: send(
                    piece(), piece(), self.team_send.at[i, k, t], self.team_recv.at[i, k, t],
                    (self.team[t], self.shard),
                )
            )
        self.push(
            lambda: send(
                piece(), piece(), self.core_send.at[i, k, 0], self.core_recv.at[i, k, 0], self.mate
            )
        )

    def own_to_mate(self, own, i):
        self.push(
            lambda: send(
                own(), self.blocks[i].at[pl.ds(self.shard * self.parts, self.parts)],
                self.core_send.at[i, 0, 0], self.core_recv.at[i, 0, 0], self.mate,
            )
        )

    def team_to_mate(self, i):
        for k in range(1, self.levels):
            for t in range(1, self.parts):

                def piece(k=k, t=t):
                    return self.blocks[i].at[self.far[k] * self.parts + self.team_part[t]]

                self.arrived(piece(), self.team_send.at[i, k, t], self.team_recv.at[i, k, t])
                self.push(
                    lambda piece=piece, k=k, t=t: send(
                        piece(), piece(), self.core_send.at[i, k, t], self.core_recv.at[i, k, t],
                        self.mate,
                    )
                )

    def mate_arrived(self, i):
        piece = self.blocks[i].at[pl.ds(self.other * self.parts, self.parts)]
        self.arrived(piece, self.core_send.at[i, 0, 0], self.core_recv.at[i, 0, 0])
        for k in range(1, self.levels):
            for t in range(self.parts):
                piece = self.blocks[i].at[self.far_other[k] * self.parts + self.team_part[t]]
                self.arrived(piece, self.core_send.at[i, k, t], self.core_recv.at[i, k, t])

    def finish(self):
        for make in self.sends:
            make().wait_send()


def gather_sems(levels, parts, count):
    dma = pltpu.SemaphoreType.DMA
    return [dma((count, levels))] * 2 + [dma((count, levels, parts))] * 4


def gather_parts(groups, rows):
    return next(p for p in (4, 2, 1) if groups % p == 0 and rows % (16 * p) == 0)


class Rows:
    def __init__(self, groups, own, outs, sems):
        self.own, self.outs = own, outs
        self.send_sem, self.recv_sem = sems
        group, self.shard = lax.axis_index("expert"), lax.axis_index("shard")
        self.team = [flipped(group, t) for t in range(groups)]
        self.near = range(1, 1 + len(outs))

    def copy(self, t):
        return send(
            self.own, self.outs[t - 1], self.send_sem.at[t], self.recv_sem.at[t],
            (self.team[t], self.shard),
        )

    def start(self):
        for t in self.near:
            self.copy(t).start()

    def finish(self):
        for t in self.near:
            self.copy(t).wait()


def gather_kernel(groups, parts, levels, *refs):
    ins, own_rows, outs, refs = refs[:2], refs[2], refs[3:5], refs[5:]
    count = 2 if groups == 4 else groups - 1
    others, refs = refs[:count], refs[count:]
    bounce, local_sem = refs[:2], refs[2]
    plan = Gather(parts, levels, outs, refs[3:9])
    rows = Rows(groups, own_rows, others, refs[9:11])
    greet(
        [plan.mate]
        + [(plan.group, plan.far[k]) for k in range(1, levels)]
        + [(rows.team[t], rows.shard) for t in range(1, groups)]
    )
    own = pl.ds(plan.shard * parts, parts)
    loads = [pltpu.make_async_copy(ins[i], bounce[i], local_sem.at[0, i]) for i in range(2)]
    stores = [pltpu.make_async_copy(bounce[i], outs[i].at[own], local_sem.at[1, i]) for i in range(2)]
    for copy in loads:
        copy.start()
    for i in range(2):
        plan.near(ins[i], i)
    rows.start()
    plan.own_to_mate(lambda: ins[0], 0)
    for load, store in zip(loads, stores):
        load.wait()
        store.start()
    for k in range(1, levels):
        plan.near_arrived(0, k)
        plan.spread(0, k)
    plan.team_to_mate(0)
    for k in range(1, levels):
        plan.near_arrived(1, k)
    plan.mate_arrived(0)
    plan.finish()
    rows.finish()
    for copy in stores:
        copy.wait()


def gather_weights(blocks, own_rows, groups, shards):
    rows = blocks[0].shape[0]
    parts = gather_parts(groups, rows)
    levels, count = shards // 2, 2 if groups == 4 else groups - 1
    blocks = [b.reshape(parts, rows // parts, b.shape[1]) for b in blocks]
    dma = pltpu.SemaphoreType.DMA
    return pl.pallas_call(
        functools.partial(gather_kernel, groups, parts, levels),
        in_specs=[pl.BlockSpec(memory_space=pl.ANY)] * 3,
        out_specs=[pl.BlockSpec(memory_space=pl.ANY)] * (2 + count),
        out_shape=[
            jax.ShapeDtypeStruct((shards * parts,) + b.shape[1:], b.dtype) for b in blocks
        ]
        + [jax.ShapeDtypeStruct(own_rows.shape, own_rows.dtype)] * count,
        scratch_shapes=[pltpu.VMEM(b.shape, b.dtype) for b in blocks]
        + [dma((2, 2))]
        + gather_sems(levels, parts, 2)
        + [dma((groups,)), dma((groups,))],
        compiler_params=pltpu.CompilerParams(
            collective_id=0, has_side_effects=True, vmem_limit_bytes=62 << 20
        ),
        name="gather_weights",
    )(*blocks, own_rows)


class Reduce:
    def __init__(self, groups, levels, cols, refs, sems):
        self.groups, self.levels, self.relay = groups, levels, groups == 4
        self.held, self.from_core, self.passing, self.from_group = refs
        self.core_send, self.core_recv, self.pass_send, self.pass_recv, self.group_send, self.group_recv = sems
        self.group, self.shard = lax.axis_index("expert"), lax.axis_index("shard")
        level, self.core = self.shard // 2, self.shard % 2
        self.mate = (self.group, self.shard + 1 - 2 * self.core)
        self.team = [flipped(self.group, t) for t in range(groups)]
        self.far = [flipped(level, k) for k in range(levels)]
        self.order = sorted(range(levels), key=lambda k: (k & -k or levels, k))
        self.near = [1, 2] if self.relay else list(range(1, groups))
        self.sends = []
        turns = ([3] if self.relay else []) + self.near + [0]
        self.even = self.held.shape[4] * groups == cols
        self.chunks = [self.team[t] if self.even else k for k, t in enumerate(turns)]

    def greet(self, climbs):
        greet(
            [self.mate]
            + [(self.group, self.far[k] * 2 + self.core) for k in range(1, self.levels) if climbs]
            + [(self.team[t], self.shard) for t in range(1, self.groups)]
        )

    def push(self, make):
        make().start()
        self.sends.append(make)

    def arrived(self, piece, send_sem, recv_sem):
        send(piece, piece, send_sem, recv_sem, self.mate).wait_recv()

    def fill(self, left, right):
        rows, chunk = self.held.shape[3:]
        tall = 768
        per = tall // rows
        even = self.even
        for k in self.chunks:
            low = k * chunk
            many = chunk if even else max(0, min(chunk, right.shape[1] - low))
            if many:
                at = pl.ds(pl.multiple_of(low, 128), many) if even else slice(low, low + many)

                @pl.loop(0, left.shape[0] // tall)
                def _(c):
                    part = pl.ds(pl.multiple_of(c * tall, tall), tall)
                    value = dot_nn(left[part, :], right[:, at]).astype(BF16)
                    for i in range(per):
                        s = c * per + i
                        self.held[k, s % 2, s // 2, :, :many] = value[i * rows : (i + 1) * rows]

            self.push(
                lambda k=k: send(
                    self.held.at[k, 1 - self.core], self.from_core.at[k],
                    self.core_send.at[k], self.core_recv.at[k], self.mate,
                )
            )

    def pass_copy(self, part, k):
        half = self.held.shape[3] // 2
        return send(
            self.held.at[self.team[3], self.core, self.far[k], pl.ds(part * half, half)],
            self.passing.at[part, k], self.pass_send.at[part, k], self.pass_recv.at[part, k],
            (self.team[1 + part], self.shard),
        )

    def group_copy(self, t, k):
        return send(
            self.held.at[self.team[t], self.core, self.far[k]], self.from_group.at[t, k],
            self.group_send.at[t, k], self.group_recv.at[t, k], (self.team[t], self.shard),
        )

    def merge(self):
        for n, k in enumerate(self.chunks):
            self.arrived(self.from_core.at[k], self.core_send.at[k], self.core_recv.at[k])

            @pl.loop(0, self.levels)
            def _(z):
                self.held[k, self.core, z] = (
                    self.held[k, self.core, z].astype(F32) + self.from_core[k, z].astype(F32)
                ).astype(BF16)

            if self.relay and n == 0:
                for j in self.order:
                    for part in range(2):
                        self.push(lambda part=part, j=j: self.pass_copy(part, j))
        if not self.relay:
            for j in self.order:
                for t in self.near:
                    self.push(lambda t=t, j=j: self.group_copy(t, j))

    def spread(self):
        if not self.relay:
            return
        half = self.held.shape[3] // 2
        for k in self.order:
            for part in range(2):
                self.arrived(
                    self.passing.at[part, k], self.pass_send.at[part, k], self.pass_recv.at[part, k]
                )
                at = pl.ds(part * half, half)
                piece = self.held.at[self.team[2 - part], self.core, self.far[k], at]
                piece[...] = (piece[...].astype(F32) + self.passing[part, k].astype(F32)).astype(BF16)
            for t in self.near:
                self.push(lambda t=t, k=k: self.group_copy(t, k))

    def collect(self, k):
        total = self.held[self.group, self.core, self.far[k]].astype(F32)
        for t in self.near:
            self.arrived(self.from_group.at[t, k], self.group_send.at[t, k], self.group_recv.at[t, k])
            total = total + self.from_group[t, k].astype(F32)
        return total

    def bits(self):
        return [bit for bit in (1, 2, 4, 8, 16) if bit < self.levels]

    def climb(self, summed, from_level, sems, bit, only=None):
        for k in range(self.levels) if only is None else [only]:
            if k & bit and not k & (bit - 1):
                self.push(
                    lambda k=k: send(
                        summed.at[k], from_level.at[k], sems[0].at[k], sems[1].at[k],
                        (self.group, self.far[bit] * 2 + self.core),
                    )
                )

    def climbed(self, summed, from_level, sems, bit):
        for k in range(self.levels):
            if k & bit and not k & (bit - 1):
                self.arrived(from_level.at[k], sems[0].at[k], sems[1].at[k])
                to = k - bit
                summed[to] = (summed[to].astype(F32) + from_level[k].astype(F32)).astype(BF16)

    def settle(self, summed, home, home_sems):
        home[self.group] = summed[0]
        for t in range(1, self.groups):
            self.push(
                lambda t=t: send(
                    home.at[self.group], home.at[self.group],
                    home_sems[0].at[t], home_sems[1].at[t], (self.team[t], self.shard),
                )
            )

    def landed(self, home, home_sems):
        for t in range(1, self.groups):
            self.arrived(home.at[self.team[t]], home_sems[0].at[t], home_sems[1].at[t])

    def finish(self):
        for make in self.sends:
            make().wait_send()


def chunk_of(total, groups):
    return 128 * (-(-total // (128 * groups)))


def reduce_buffers(groups, levels, rows, chunk):
    piece = (rows, chunk)
    passing = (2, levels, rows // 2, chunk) if groups == 4 else (1, 1, 16, 128)
    return [
        pltpu.VMEM((groups, 2, levels) + piece, BF16),
        pltpu.VMEM((groups, levels) + piece, BF16),
        pltpu.VMEM(passing, BF16),
        pltpu.VMEM((groups, levels) + piece, BF16),
    ]


def reduce_sems(groups, levels):
    dma = pltpu.SemaphoreType.DMA
    return [dma((groups,))] * 2 + [dma((2, levels))] * 2 + [dma((groups, levels))] * 2


class FewRows:
    def __init__(self, plan, refs, sems):
        self.plan = plan
        self.rows, self.from_core, self.from_group, self.pieces, self.from_level = refs
        self.core_send, self.core_recv, self.group_send, self.group_recv, self.level_send, self.level_recv = sems

    def start(self):
        plan = self.plan
        plan.push(
            lambda: send(self.rows, self.from_core, self.core_send, self.core_recv, plan.mate)
        )

    def over_groups(self):
        plan = self.plan
        plan.arrived(self.from_core, self.core_send, self.core_recv)
        total = self.rows[...].astype(F32) + self.from_core[...].astype(F32)
        self.from_group[plan.group] = total.astype(BF16)
        for t in range(1, plan.groups):
            plan.push(
                lambda t=t: send(
                    self.from_group.at[plan.group], self.from_group.at[plan.group],
                    self.group_send.at[t], self.group_recv.at[t], (plan.team[t], plan.shard),
                )
            )

    def over_levels(self):
        plan = self.plan
        for t in range(1, plan.groups):
            plan.arrived(self.from_group.at[plan.team[t]], self.group_send.at[t], self.group_recv.at[t])
        total = self.from_group[0].astype(F32)
        for g in range(1, plan.groups):
            total = total + self.from_group[g].astype(F32)
        wide = self.pieces.shape[2]
        for s in range(2 * plan.levels):
            self.pieces[s] = total[:, s * wide : (s + 1) * wide].astype(BF16)
        for k in range(1, plan.levels):
            plan.push(
                lambda k=k: send(
                    self.pieces.at[plan.far[k] * 2 + plan.core], self.from_level.at[k],
                    self.level_send.at[k], self.level_recv.at[k],
                    (plan.group, plan.far[k] * 2 + plan.core),
                )
            )

    def total(self):
        plan = self.plan
        total = self.pieces[plan.shard].astype(F32)
        for k in range(1, plan.levels):
            plan.arrived(self.from_level.at[k], self.level_send.at[k], self.level_recv.at[k])
            total = total + self.from_level[k].astype(F32)
        return total


def input_back(dproj_ref, w_ref, x_ref, gain_ref, held, inner, scale, gain_grad):
    width, step = x_ref.shape[1], 256
    x = x_ref[...].astype(F32)
    scale[...] = lax.rsqrt(jnp.mean(x * x, axis=-1, keepdims=True) + EPSILON)
    inner[...] = jnp.zeros(inner.shape, F32)

    @pl.loop(0, width // step)
    def _(c):
        at = pl.ds(pl.multiple_of(c * step, step), step)
        normed_grads = dot_nt(dproj_ref[...], w_ref[at, :])
        x = x_ref[:, at].astype(F32)
        weighted = normed_grads * gain_ref[:, at].astype(F32)
        inner[...] += jnp.sum(weighted * x, axis=-1, keepdims=True)
        gain_grad[:, at] = jnp.sum(normed_grads * x * scale[...], axis=0, keepdims=True)
        r = scale[...]
        held[:, at] += r * weighted

    r = scale[...]
    factor = r * r * r * (inner[...] * (1.0 / width))
    for low in range(0, width, step):
        cols = slice(low, low + step)
        held[:, cols] -= x_ref[:, cols].astype(F32) * factor


def reduce_kernel(groups, levels, *refs):
    normed_t, dproj_ref, gain_two_ref, router_ref, out_sum_ref, gain_ref = refs[:6]
    w_in, x_in, hidden_grads_in, *refs = refs[6:]
    count = 2 if groups == 4 else groups - 1
    out_sent, refs = refs[:count], refs[count:]
    out_ref, qkv_ref, misc_ref, input_grad_ref, *refs = refs
    out_came, refs = refs[:count], refs[count:]
    summed, from_level, home, out_summed, out_level, out_home = refs[:6]
    plan = Reduce(groups, levels, dproj_ref.shape[1], refs[6:10], refs[10:16])
    level_sems, home_sems, out_level_sems, out_home_sems = (refs[i : i + 2] for i in range(16, 24, 2))
    misc = FewRows(plan, refs[24:29], refs[29:35])
    w_buf, x_buf, held, inner, scale, gain_grad, load_sem, store_sem, row_send, row_recv = refs[35:]
    loads = [
        pltpu.make_async_copy(w_in.at[:, : dproj_ref.shape[1]], w_buf, load_sem.at[0]),
        pltpu.make_async_copy(x_in, x_buf, load_sem.at[1]),
        pltpu.make_async_copy(hidden_grads_in, held, load_sem.at[2]),
    ]
    for load in loads:
        load.start()
    first, *others = plan.bits()
    plan.greet(True)
    out_summed[...] = out_sum_ref[...]
    plan.climb(out_summed, out_level, out_level_sems, first)
    plan.fill(normed_t, dproj_ref)
    plan.merge()
    plan.spread()
    plan.climbed(out_summed, out_level, out_level_sems, first)
    for bit in others[:1]:
        plan.climb(out_summed, out_level, out_level_sems, bit)
    for k in plan.order:
        summed[k] = plan.collect(k).astype(BF16)
        plan.climb(summed, from_level, level_sems, first, k)
    row_copies = [
        send(
            out_sent[t - 1], out_came[t - 1], row_send.at[t], row_recv.at[t],
            (plan.team[t], plan.shard),
        )
        for t in range(1, count + 1)
    ]
    for copy in row_copies:
        copy.start()
    for load in loads:
        load.wait()
    input_back(dproj_ref, w_buf, x_buf, gain_ref, held, inner, scale, gain_grad)
    store = pltpu.make_async_copy(held, input_grad_ref, store_sem)
    store.start()
    experts = router_ref.shape[0]
    gains = jnp.concatenate(
        [gain_grad[...], gain_two_ref[...], jnp.zeros((6, gain_grad.shape[1]), F32)], axis=0
    )
    misc.rows[...] = jnp.zeros(misc.rows.shape, BF16)
    misc.rows[:8] = gains.astype(BF16)
    misc.rows[8 : 8 + experts] = router_ref[...].astype(BF16)
    misc.start()
    misc.over_groups()
    for n, bit in enumerate(others):
        plan.climbed(out_summed, out_level, out_level_sems, bit)
        for bit in others[n + 1 : n + 2]:
            plan.climb(out_summed, out_level, out_level_sems, bit)
    plan.settle(out_summed, out_home, out_home_sems)
    plan.climbed(summed, from_level, level_sems, first)
    for bit in others[:1]:
        plan.climb(summed, from_level, level_sems, bit)
    misc.over_levels()
    for n, bit in enumerate(others):
        plan.climbed(summed, from_level, level_sems, bit)
        for bit in others[n + 1 : n + 2]:
            plan.climb(summed, from_level, level_sems, bit)
    plan.settle(summed, home, home_sems)
    misc_ref[...] = misc.total()
    plan.landed(out_home, out_home_sems)
    out_ref[...] = out_home[...]
    plan.landed(home, home_sems)
    qkv_ref[...] = home[...]
    plan.finish()
    store.wait()
    for copy in row_copies:
        copy.wait()


def reduce_weights(normed_t, dproj, gain_two, router, out_sum, gain_row, w_full, x, hidden_grads, out_sent, groups, shards):
    tokens, width = x.shape
    levels, rows = shards // 2, width // shards
    total = dproj.shape[1]
    chunk, out_chunk = chunk_of(total, groups), out_sum.shape[2]
    dma = pltpu.SemaphoreType.DMA
    vmem, anywhere = (pl.BlockSpec(memory_space=m) for m in (pltpu.VMEM, pl.ANY))
    whole, out_whole = (groups, rows, chunk), (groups, rows, out_chunk)
    few = 16 * (-(-(8 + router.shape[0]) // 16))
    return pl.pallas_call(
        functools.partial(reduce_kernel, groups, levels),
        in_specs=[vmem] * 6 + [anywhere] * (3 + len(out_sent)),
        out_specs=[vmem] * 3 + [anywhere] * (1 + len(out_sent)),
        out_shape=[jax.ShapeDtypeStruct(s, BF16) for s in (out_whole, whole)]
        + [jax.ShapeDtypeStruct((few, rows), F32), jax.ShapeDtypeStruct((tokens, width), F32)]
        + [jax.ShapeDtypeStruct(o.shape, o.dtype) for o in out_sent],
        scratch_shapes=[
            pltpu.VMEM((levels, rows, chunk), BF16),
            pltpu.VMEM((levels, rows, chunk), BF16),
            pltpu.VMEM(whole, BF16),
            pltpu.VMEM((levels, rows, out_chunk), BF16),
            pltpu.VMEM((levels, rows, out_chunk), BF16),
            pltpu.VMEM(out_whole, BF16),
        ]
        + reduce_buffers(groups, levels, rows, chunk)
        + reduce_sems(groups, levels)
        + [dma((levels,))] * 2 + [dma((groups,))] * 2 + [dma((levels,))] * 2 + [dma((groups,))] * 2
        + [
            pltpu.VMEM((few, width), BF16),
            pltpu.VMEM((few, width), BF16),
            pltpu.VMEM((groups, few, width), BF16),
            pltpu.VMEM((shards, few, rows), BF16),
            pltpu.VMEM((levels, few, rows), BF16),
            dma, dma, dma((groups,)), dma((groups,)), dma((levels,)), dma((levels,)),
            pltpu.VMEM((width, total), BF16),
            pltpu.VMEM((tokens, width), BF16),
            pltpu.VMEM((tokens, width), F32),
            pltpu.VMEM((tokens, 1), F32),
            pltpu.VMEM((tokens, 1), F32),
            pltpu.VMEM((1, width), F32),
            dma((3,)), dma, dma((groups,)), dma((groups,)),
        ],
        compiler_params=pltpu.CompilerParams(
            collective_id=1, has_side_effects=True, vmem_limit_bytes=62 << 20
        ),
        cost_estimate=pl.CostEstimate(
            flops=2 * tokens * width * total, bytes_accessed=8 << 20, transcendentals=0
        ),
        name="reduce_weights",
    )(normed_t, dproj, gain_two, router, out_sum, gain_row, w_full, x, hidden_grads, *out_sent)


def expert_kernel(capacity, shards, groups, count, base, stage, *refs):
    refs = list(refs)
    take = lambda n: [refs.pop(0) for _ in range(n)]
    if stage == "first":
        x_own, meta_own = take(2)
        u_ins = take(3 if groups == 4 else groups)
    else:
        x_ref, u_ref, meta_ref, out_in, dx_in, gg_in = take(6)
    packed_ref = take(1)[0]
    if stage == "last":
        earlier_ref = take(1)[0]
    if stage == "first":
        x_all, u_all, meta_all, out_ref, dx_ref, gg_ref, dw_out = take(7)
    elif stage == "last":
        out_homes = take(3 if groups == 4 else groups)
        dx_home, gg_home, dw_out = take(3)
    else:
        out_ref, dx_ref, gg_ref, dw_out = take(4)
    xs, us, bs, inn, dw, dw_sem, we_all, wp_all, we_sem, wp_sem = take(10)
    if stage != "between":
        core_buf, core_send, core_recv, credit = take(4)
    if stage == "first":
        x_buf, u_buf, meta_buf = take(3)
        x_send, x_recv, meta_send, meta_recv, load_sem, u_sem, meta_sem, keep_sem, pass_sem = take(9)
    elif stage == "last":
        buf, passing, gg_buf = take(3)
        load_sem, pass_send, pass_recv, dx_send, dx_recv, gg_send, gg_recv, keep_sem = take(8)
    turn_at, expert = pl.program_id(0), pl.program_id(1)
    last_turn, last = groups - 1, count - 1
    group, shard = lax.axis_index("expert"), lax.axis_index("shard")
    team = [flipped(group, t) for t in range(groups)]
    core = shard % 2
    mate = (group, shard + 1 - 2 * core)
    width = xs.shape[2]
    tokens = x_buf.shape[0] if stage == "first" else x_ref.shape[1]
    tall, short = width // shards, FF // shards
    side = width - 2 * FF
    we_ref, wp_ref = we_all.at[expert], wp_all.at[expert]

    @pl.when((turn_at == 0) & (expert == 0))
    def _():
        for e in range(count):

            @pl.loop(0, shards)
            def _(s):
                a = pl.ds(pl.multiple_of(s * tall, 16), tall)
                b = pl.ds(pl.multiple_of(s * short, 16), short)
                low = pl.ds(pl.multiple_of(s * short, 16), short // 2)
                high = pl.ds(pl.multiple_of(s * short + short // 2, 16), short // 2)
                source = packed_ref.at[s, e]
                rest = pl.ds(tall + short, short // 2)
                for piece, target, sem in (
                    (source.at[:tall], we_all.at[e, a], we_sem),
                    (source.at[tall : tall + short], wp_all.at[e, b, : 2 * FF], wp_sem),
                    (source.at[rest, :side], wp_all.at[e, low, 2 * FF :], wp_sem),
                    (source.at[rest, side:], wp_all.at[e, high, 2 * FF :], wp_sem),
                ):
                    pltpu.make_async_copy(piece, target, sem.at[e]).start()

    def core_copy(source):
        return send(source.at[:, 1 - core], core_buf, core_send, core_recv, mate)

    def core_add(source):
        core_copy(source).wait()

        @pl.loop(0, shards // 2)
        def _(z):
            core_buf[z] = (dw[z, core].astype(F32) + core_buf[z].astype(F32)).astype(BF16)

    def store_half(at):
        return pltpu.make_async_copy(core_buf, dw_out.at[:, at], dw_sem)

    def core_free(at):
        store_half(at).wait()
        pl.semaphore_signal(credit, inc=1, device_id=mate, device_id_type=pl.DeviceIdType.MESH)

    def own_half():
        return pltpu.make_async_copy(earlier_ref.at[:, core], dw.at[:, core], keep_sem.at[1])

    before = 1 if stage == "last" else 0

    if stage == "first":
        relay = groups == 4
        near = [1, 2] if relay else list(range(1, groups))
        half = tokens // 2

        def x_copy(t):
            return send(x_own, x_all.at[t], x_send.at[t], x_recv.at[t], (team[t], shard))

        def passed(source, target, part, sems):
            at = pl.ds(part * half, half)
            return send(
                source.at[at], target.at[3, at], sems.at[0, part], sems.at[1, part],
                (team[2 - part], shard),
            )

        def x_pass(part):
            return passed(x_all.at[1 + part], x_all, part, pass_sem.at[0])

        def u_pass(part):
            return passed(u_ins[1 + part], u_all, part, pass_sem.at[1])

        def meta_copy(t):
            return send(
                meta_own.at[team[t]], meta_all.at[t], meta_send.at[t], meta_recv.at[t], (team[t], shard)
            )

        def u_load(t):
            source = u_all.at[t] if relay and t == 3 else u_ins[t]
            return pltpu.make_async_copy(source, u_buf.at[t % 2], u_sem.at[t % 2])

        def x_keep():
            return pltpu.make_async_copy(x_buf, x_all.at[0], keep_sem.at[0])

        def meta_keep():
            return pltpu.make_async_copy(meta_buf, meta_all.at[0], keep_sem.at[1])

        def u_keep(t):
            return pltpu.make_async_copy(u_buf.at[t % 2], u_all.at[t], keep_sem.at[2 + t])

        for t in range(groups):

            @pl.when((turn_at == t) & (expert == 0))
            def _():
                if t == 0:
                    u_load(0).start()
                    greet([mate] + [(team[k], shard) for k in range(1, groups)])
                    for k in range(1, groups):
                        meta_copy(k).start()
                    for k in near:
                        x_copy(k).start()
                    fetch_x, fetch_meta = x_own, meta_own.at[group]
                else:
                    if not relay:
                        x_copy(t).wait_recv()
                    elif t == 1:
                        for k in near:
                            x_copy(k).wait_recv()
                        for part in range(2):
                            x_pass(part).start()
                        for part in range(2):
                            u_pass(part).start()
                    elif t == 3:
                        for part in range(2):
                            x_pass(part).wait_recv()
                            u_pass(part).wait_recv()
                        u_load(3).start()
                    meta_copy(t).wait_recv()
                    u_keep(t - 1).wait()
                    if t == 1:
                        x_keep().wait()
                        meta_keep().wait()
                    fetch_x, fetch_meta = x_all.at[t], meta_all.at[t]
                load = pltpu.make_async_copy(fetch_x, x_buf, load_sem)
                load_meta = pltpu.make_async_copy(fetch_meta, meta_buf, meta_sem)
                load.start()
                load_meta.start()
                if t + 1 < groups and not (relay and t == 2):
                    u_load(t + 1).start()
                u_load(t).wait()
                load_meta.wait()
                load.wait()
                if not (relay and t == 3):
                    u_keep(t).start()
                if t == 0:
                    x_keep().start()
                    meta_keep().start()

        x_now, u_now, meta_now = x_buf, u_buf.at[turn_at % 2], meta_buf
    else:
        x_now, u_now, meta_now = x_ref.at[0], u_ref.at[0], meta_ref.at[0]

    if stage == "last":
        relay = groups == 4
        slots, half = buf.shape[1], tokens // 2
        halves = [pl.ds(0, half), pl.ds(half, half)]

        def kept(kind, i):
            return buf.at[kind, i % slots]

        def load(kind, i):
            source = dx_in if kind else out_in
            return pltpu.make_async_copy(
                source.at[last_turn - i], kept(kind, i), load_sem.at[kind, i % 2]
            )

        def store(i):
            return pltpu.make_async_copy(kept(0, i), out_homes[last_turn - i], keep_sem.at[2 + i])

        def pass_copy(kind, part):
            return send(
                kept(kind, 0).at[halves[part]], passing.at[kind, part],
                pass_send.at[kind, part], pass_recv.at[kind, part], (team[1 + part], shard),
            )

        def dx_copy(i):
            t = last_turn - i
            return send(kept(1, i), dx_home.at[t], dx_send.at[t], dx_recv.at[t], (team[t], shard))

        def dx_half(part):
            at = halves[part]
            return send(
                kept(1, 1).at[at], dx_home.at[2, at], dx_send.at[2 + part], dx_recv.at[2 + part],
                (team[2], shard),
            )

        def gg_copy(i):
            t = last_turn - i
            return send(gg_buf.at[i], gg_home.at[group], gg_send.at[t], gg_recv.at[t], (team[t], shard))

        def own_copies():
            return [
                pltpu.make_async_copy(kept(1, last_turn), dx_home.at[0], keep_sem.at[0]),
                pltpu.make_async_copy(gg_buf.at[last_turn], gg_home.at[group], keep_sem.at[1]),
            ]

        for i in range(groups):

            @pl.when((turn_at == i) & (expert == 0))
            def _():
                if i == 0:
                    for kind in range(2):
                        load(kind, 0).start()
                    greet([mate] + [(team[k], shard) for k in range(1, groups)])
                    core_copy(earlier_ref).start()
                    own_half().start()
                if i == 1:
                    own_half().wait()
                    core_add(earlier_ref)
                    store_half(0).start()
                if i == 2:
                    core_free(0)
                if i + 1 < groups:
                    if i + 1 >= slots:
                        dx_copy(i + 1 - slots).wait_send()
                        store(i + 1 - slots).wait()
                    for kind in range(2):
                        load(kind, i + 1).start()
                for kind in range(2):
                    load(kind, i).wait()

        at_now = turn_at % slots
        out_now, dx_now, gg_now = buf.at[0, at_now], buf.at[1, at_now], gg_buf.at[turn_at]
    else:
        out_now, dx_now, gg_now = out_ref.at[0], dx_ref.at[0], gg_ref.at[0]

    @pl.when(expert == 0)
    def _():
        if stage == "first":
            out_now[...] = jnp.zeros((tokens, width), BF16)
            dx_now[...] = jnp.zeros((tokens, width), BF16)
            gg_now[...] = jnp.zeros((8, tokens), F32)
        else:
            gg_now[...] = gg_in[0]
        if stage == "between":
            out_now[...] = out_in[0]
            dx_now[...] = dx_in[0]

    @pl.when(turn_at == 0)
    def _():
        pltpu.make_async_copy(we_ref, we_ref, we_sem.at[expert]).wait()
        pltpu.make_async_copy(wp_ref, wp_ref, wp_sem.at[expert]).wait()

    slot_row = meta_now[pl.ds(base + expert, 1), :]
    gate_row = meta_now[pl.ds(8 + base + expert, 1), :]
    index = lax.broadcasted_iota(jnp.int32, (capacity, tokens), 0).astype(F32)
    pick = jnp.where(index == slot_row, 1.0, 0.0)
    gate_col = jnp.sum(pick * gate_row, axis=1, keepdims=True)
    place = pick.astype(BF16)
    rows = pl.ds(pl.multiple_of(turn_at * capacity, capacity), capacity)
    x = dot_nn(place, x_now[...]).astype(BF16)
    xs[expert, rows, :] = x
    u_rows = dot_nn(place, u_now[...]).astype(BF16)
    us[expert, rows, :] = u_rows
    both_parts = dot_nn(x, we_ref[...])
    gate, up = both_parts[:, :FF], both_parts[:, FF:]
    back = dot_nt(u_rows, wp_ref[...])
    sig = 1.0 / (1.0 + jnp.exp(-gate))
    act = gate * sig
    inner = act * up
    inner_low = inner.astype(BF16)
    gate_grad = jnp.sum(inner * back, axis=1, keepdims=True)
    here = lax.broadcasted_iota(jnp.int32, (8, tokens), 0) == base + expert
    gg_now[...] = jnp.where(here, jnp.sum(pick * gate_grad, axis=0, keepdims=True), gg_now[...])
    inn[expert, rows, :] = (inner * gate_col).astype(BF16)
    inner_grads = back * gate_col
    bs[expert, rows, :FF] = (inner_grads * up * sig * (1.0 + gate * (1.0 - sig))).astype(BF16)
    bs[expert, rows, FF:] = (inner_grads * act).astype(BF16)
    both = bs[expert, rows, :]
    weighted_t = (pick * gate_row).astype(BF16).T
    place_t = place.T
    result = dot_nn(inner_low, wp_ref[...]).astype(BF16)
    out_now[...] = (out_now[...].astype(F32) + dot_nn(weighted_t, result)).astype(BF16)
    row_grads = dot_nt(both, we_ref[...]).astype(BF16)
    dx_now[...] = (dx_now[...].astype(F32) + dot_nn(place_t, row_grads)).astype(BF16)

    if stage == "last":

        def add_passed(kind):
            for part in range(2):
                pass_copy(kind, part).wait_recv()
                target = kept(kind, 1 + part).at[halves[part]]
                target[...] = (target[...].astype(F32) + passing[kind, part].astype(F32)).astype(BF16)

        for i in range(groups):

            @pl.when((turn_at == i) & (expert == last))
            def _():
                if i < last_turn:
                    gg_copy(i).start()
                else:
                    for copy in own_copies():
                        copy.start()
                if not relay:
                    store(i).start()
                    if i < last_turn:
                        dx_copy(i).start()
                elif i == 0:
                    for kind in (1, 0):
                        for part in range(2):
                            pass_copy(kind, part).start()
                elif i == 1:
                    dx_half(1).start()
                elif i == 2:
                    add_passed(1)
                    dx_copy(2).start()
                    dx_half(0).start()
                else:
                    add_passed(0)
                    for k in range(1, groups):
                        store(k).start()

    @pl.when(turn_at == last_turn)
    def _():
        if stage != "between" and count > 1:

            @pl.when(expert > 0)
            def _():
                core_add(dw)
                store_half(before + expert - 1).start()

        wide, half = 384, FF // 2

        @pl.loop(0, width // wide)
        def _(c):
            at = pl.ds(pl.multiple_of(c * wide, wide), wide)
            value = dot_tn(xs[expert, :, at], bs[expert]).astype(BF16)
            for i in range(wide // tall):
                s = c * (wide // tall) + i
                dw[s // 2, s % 2, :tall, :] = value[i * tall : (i + 1) * tall]

        @pl.loop(0, FF // half)
        def _(c):
            at = pl.ds(pl.multiple_of(c * half, half), half)
            value = dot_tn(inn[expert, :, at], us[expert]).astype(BF16)
            for i in range(half // short):
                s, low = c * (half // short) + i, i * short
                mid, high = low + short // 2, low + short
                dw[s // 2, s % 2, tall : tall + short, :] = value[low:high, : 2 * FF]
                dw[s // 2, s % 2, tall + short :, :side] = value[low:mid, 2 * FF :]
                dw[s // 2, s % 2, tall + short :, side:] = value[mid:high, 2 * FF :]

        if stage == "between":
            pltpu.make_async_copy(dw, dw_out, dw_sem).start()
        else:
            if count > 1:

                @pl.when(expert > 0)
                def _():
                    core_free(before + expert - 1)

            if before:
                pl.semaphore_wait(credit, 1)
            else:

                @pl.when(expert > 0)
                def _():
                    pl.semaphore_wait(credit, 1)

            core_copy(dw).start()

    @pl.when((turn_at == last_turn) & (expert == last))
    def _():
        if stage == "between":
            pltpu.make_async_copy(dw, dw_out, dw_sem).wait()
        else:
            core_add(dw)
            store_half(before + last).start()
            store_half(before + last).wait()
        if stage == "first":
            if not relay:
                u_keep(last_turn).wait()
            for t in range(1, groups):
                meta_copy(t).wait_send()
            for t in near:
                x_copy(t).wait_send()
            if relay:
                for part in range(2):
                    x_pass(part).wait_send()
                    u_pass(part).wait_send()
        if stage == "last":
            for i in range(groups - 1):
                t = last_turn - i
                gg_copy(i).wait_send()
                send(
                    gg_buf.at[i], gg_home.at[team[t]], gg_send.at[t], gg_recv.at[t], (team[t], shard)
                ).wait_recv()
            if relay:
                for part in range(2):
                    dx_half(part).wait()
                    for kind in range(2):
                        pass_copy(kind, part).wait_send()
                dx_copy(2).wait()
                for k in range(1, groups):
                    store(k).wait()
            else:
                for i in range(groups - 1):
                    if i + slots >= groups:
                        dx_copy(i).wait_send()
                    dx_copy(i).wait_recv()
                for i in range(groups - slots, groups):
                    store(i).wait()
            for copy in own_copies():
                copy.wait()


def expert_call(capacity, shards, groups, base, stage, data, packed_weights, *kept):
    count = packed_weights.shape[1]
    tokens, width = data[0].shape[-2:]
    total = groups * capacity
    anywhere = pl.BlockSpec(memory_space=pl.ANY)
    turned = (lambda i: i) if stage == "first" else (lambda i: groups - 1 - i)
    block = pl.BlockSpec((1, tokens, width), lambda i, e: (turned(i), 0, 0))
    small = pl.BlockSpec((1, 8, tokens), lambda i, e: (turned(i), 0, 0))
    dma = pltpu.SemaphoreType.DMA
    many = jax.ShapeDtypeStruct((groups, tokens, width), BF16)
    grads = jax.ShapeDtypeStruct((groups, 8, tokens), F32)
    piece = ((width + FF + FF // 2) // shards, 2 * FF)
    summed = 2 if stage == "between" else count + len(kept)
    weights = jax.ShapeDtypeStruct((shards // 2, summed) + piece, BF16)
    meta = jax.ShapeDtypeStruct((groups, 16, tokens), F32)
    scratch = [
        pltpu.VMEM((count, total, width), BF16),
        pltpu.VMEM((count, total, width), BF16),
        pltpu.VMEM((count, total, 2 * FF), BF16),
        pltpu.VMEM((count, total, FF), BF16),
        pltpu.VMEM((shards // 2, 2) + piece, BF16),
        dma,
        pltpu.VMEM((count, width, 2 * FF), BF16),
        pltpu.VMEM((count, FF, width), BF16),
        dma((count,)), dma((count,)),
    ]
    if stage != "between":
        scratch += [
            pltpu.VMEM((shards // 2,) + piece, BF16), dma, dma, pltpu.SemaphoreType.REGULAR,
        ]
    if stage == "first":
        in_specs = [anywhere] * len(data)
        out_specs = [anywhere] * 3 + [block, block, small, anywhere]
        out_shape = [many, many, meta, many, many, grads, weights]
        scratch += [
            pltpu.VMEM((tokens, width), BF16),
            pltpu.VMEM((2, tokens, width), BF16),
            pltpu.VMEM((16, tokens), F32),
            dma((groups,)), dma((groups,)), dma((groups,)), dma((groups,)),
            dma, dma((2,)), dma, dma((2 + groups,)), dma((2, 2, 2)),
        ]
    else:
        meta_block = pl.BlockSpec((1, 16, tokens), lambda i, e: (turned(i), 0, 0))
        in_specs = [block, block, meta_block, block, block, small]
        out_specs = [block, block, small, anywhere]
        if stage == "last":
            in_specs[3:5] = [anywhere] * 2
            sources = 3 if groups == 4 else groups
            out_specs = [anywhere] * (3 + sources)
            slots = groups if groups == 4 else 3
            passed = 2 if groups == 4 else 1
            scratch += [
                pltpu.VMEM((2, slots, tokens, width), BF16),
                pltpu.VMEM((passed, passed, tokens // 2, width), BF16),
                pltpu.VMEM((groups, 8, tokens), F32),
                dma((2, 2)), dma((2, 2)), dma((2, 2)),
                dma((groups,)), dma((groups,)), dma((groups,)), dma((groups,)), dma((2 + groups,)),
            ]
        out_shape = [many, many, grads, weights]
        if stage == "last":
            out_shape[:1] = [jax.ShapeDtypeStruct((tokens, width), BF16)] * sources
    remote = {"first": 2, "last": 3}
    return pl.pallas_call(
        functools.partial(expert_kernel, capacity, shards, groups, count, base, stage),
        grid=(groups, count),
        in_specs=in_specs + [anywhere] * (1 + len(kept)),
        out_specs=out_specs,
        out_shape=out_shape,
        scratch_shapes=scratch,
        compiler_params=pltpu.CompilerParams(
            vmem_limit_bytes=62 << 20,
            **({"collective_id": remote[stage], "has_side_effects": True} if stage in remote else {}),
        ),
        cost_estimate=pl.CostEstimate(
            flops=2 * count * total * width * (4 * tokens + 9 * FF),
            bytes_accessed=6 * groups * tokens * width * 2,
            transcendentals=count * total * FF,
        ),
        name="experts_" + stage,
    )(*data, packed_weights, *kept)


def norm_back(values, gain_row, grad_rows):
    scale_rows = lax.rsqrt(jnp.mean(values * values, axis=-1, keepdims=True) + EPSILON)
    weighted = gain_row * grad_rows
    inner_mean = jnp.mean(weighted * values, axis=-1, keepdims=True)
    input_part = (
        scale_rows * weighted - values * (scale_rows * scale_rows * scale_rows) * inner_mean
    )
    gain_part = jnp.sum(grad_rows * values * scale_rows, axis=0)
    return (input_part, gain_part)


def pack_kernel(
    cuts, expand_ref, project_ref, qkv_ref, gain_one_ref, gain_two_ref, router_ref, packed_ref, *refs
):
    *outs, misc = refs
    short = project_ref.shape[1]
    tall = expand_ref.shape[1]
    side = project_ref.shape[2] - 2 * FF
    for (low, high), out in zip(cuts, outs):
        for e in range(low, high):
            out[e - low, :tall] = expand_ref[e]
            out[e - low, tall : tall + short] = project_ref[e, :, : 2 * FF]
            out[e - low, tall + short :, :side] = project_ref[e, : short // 2, 2 * FF :]
            out[e - low, tall + short :, side:] = project_ref[e, short // 2 :, 2 * FF :]
    for j in range(PAIRS):
        at, to = HEADS * HEAD + j * KW, j * BLOCK + QW
        packed_ref[:, j * BLOCK : to] = qkv_ref[:, j * QW : (j + 1) * QW]
        packed_ref[:, to : to + KW] = qkv_ref[:, at : at + KW]
        at += KV_HEADS * HEAD
        packed_ref[:, to + KW : to + 2 * KW] = qkv_ref[:, at : at + KW]
    misc[...] = jnp.zeros(misc.shape, F32)
    misc[0:1] = gain_one_ref[...].astype(F32)[None]
    misc[1:2] = gain_two_ref[...].astype(F32)[None]
    misc[8 : 8 + router_ref.shape[0]] = router_ref[...].astype(F32)
    packed_ref[:, PAIRS * BLOCK :] = misc[...].T.astype(BF16)


def pack_weights(expand, project, qkv, gain_one, gain_two, router):
    cuts = bands(expand.shape[0])
    rows = expand.shape[1] + project.shape[1] + project.shape[1] // 2
    return pl.pallas_call(
        functools.partial(pack_kernel, cuts),
        out_shape=[jax.ShapeDtypeStruct((qkv.shape[0], PAIRS * BLOCK + MISC), BF16)]
        + [jax.ShapeDtypeStruct((high - low, rows, 2 * FF), BF16) for low, high in cuts],
        scratch_shapes=[pltpu.VMEM((MISC, qkv.shape[0]), F32)],
        compiler_params=pltpu.CompilerParams(vmem_limit_bytes=62 << 20),
        name="pack_weights",
    )(expand, project, qkv, gain_one, gain_two, router.T)


def hidden_back_kernel(
    dx_ref, gg_ref, gates_ref, router_ref, hidden_ref, gain_ref, up_ref, ffn_ref,
    grads_ref, low_ref, router_grad_ref, gain_grad_ref,
):
    gates, groups = gates_ref[...], gg_ref.shape[0]
    count = gates.shape[0] // groups
    gate_grads = jnp.concatenate([gg_ref[g, :count] for g in range(groups)], axis=0)
    mean = jnp.sum(gates * gate_grads, axis=0, keepdims=True)
    logit_grads = (gates * (gate_grads - mean)).astype(BF16)
    ffn_grads = dot_tn(logit_grads, router_ref[...])
    for g in range(dx_ref.shape[0]):
        ffn_grads = ffn_grads + dx_ref[g].astype(F32)
    hidden = hidden_ref[...]
    part, gain_part = norm_back(hidden, gain_ref[...].astype(F32), ffn_grads)
    hidden_grads = up_ref[...].astype(F32) + part
    grads_ref[...] = hidden_grads
    low_ref[...] = hidden_grads.astype(BF16)
    router_part = dot_nn(logit_grads, ffn_ref[...])

    @pl.when(pl.program_id(0) == 0)
    def _():
        router_grad_ref[...] = router_part
        gain_grad_ref[...] = gain_part[None]

    @pl.when(pl.program_id(0) > 0)
    def _():
        router_grad_ref[...] += router_part
        gain_grad_ref[...] += gain_part[None]


def hidden_back(sources, dx_home, gg_home, gates, router_rows, hidden, gain_row, out_grad, ffn_in):
    groups, tokens, width = dx_home.shape
    experts = gates.shape[0]
    step = 128
    rows = pl.BlockSpec((step, width), lambda i: (i, 0))
    return pl.pallas_call(
        hidden_back_kernel,
        grid=(tokens // step,),
        in_specs=[
            pl.BlockSpec((sources, step, width), lambda i: (0, i, 0)),
            pl.BlockSpec((groups, 8, step), lambda i: (0, 0, i)),
            pl.BlockSpec((experts, step), lambda i: (0, i)),
            whole_spec((experts, width)),
            rows,
            whole_spec((1, width)),
            rows,
            rows,
        ],
        out_specs=[rows, rows, whole_spec((experts, width)), whole_spec((1, width))],
        out_shape=[
            jax.ShapeDtypeStruct((tokens, width), F32),
            jax.ShapeDtypeStruct((tokens, width), BF16),
            jax.ShapeDtypeStruct((experts, width), F32),
            jax.ShapeDtypeStruct((1, width), F32),
        ],
        compiler_params=pltpu.CompilerParams(vmem_limit_bytes=62 << 20),
        cost_estimate=pl.CostEstimate(flops=10**8, bytes_accessed=20 << 20, transcendentals=0),
        name="hidden_back",
    )(dx_home, gg_home, gates, router_rows, hidden, gain_row, out_grad, ffn_in)


def unpack_experts(tall, short, held, expand_ref, project_ref):
    side = project_ref.shape[2] - 2 * FF
    for i in range(held.shape[0]):
        value = held[i].astype(F32)
        expand_ref[i] = value[:tall]
        project_ref[i, :, : 2 * FF] = value[tall : tall + short]
        project_ref[i, : short // 2, 2 * FF :] = value[tall + short :, :side]
        project_ref[i, short // 2 :, 2 * FF :] = value[tall + short :, side:]


def unpack_kernel(tall, short, counts, *refs):
    first_ref, last_ref, hidden_ref, *refs = refs
    others, refs = refs[: counts[2]], refs[counts[2] :]
    grad_in, *refs = refs
    out_ref, qkv_ref, few_ref, output_ref, grad_ref, expand_ref, project_ref = refs[:7]
    out_grad_ref, qkv_grad_ref, gain_one_ref, gain_two_ref, router_ref = refs[7:]
    i = pl.program_id(0)

    @pl.when(i < counts[0])
    def _():
        unpack_experts(tall, short, first_ref, expand_ref, project_ref)

    @pl.when(i >= counts[0])
    def _():
        unpack_experts(tall, short, last_ref, expand_ref, project_ref)

    @pl.when(i < 4)
    def _():
        total = hidden_ref[...]
        for other in others:
            total = total + other[...].astype(F32)
        output_ref[...] = total.astype(BF16)
        grad_ref[...] = grad_in[...]

        tile = 128
        chunk = out_ref.shape[2]
        for at in range(0, out_grad_ref.shape[1], tile):
            out_grad_ref[:, at : at + tile] = out_ref[
                at // chunk, :, at % chunk : at % chunk + tile
            ].astype(F32)
        chunk = qkv_ref.shape[2]
        for at in range(0, qkv_grad_ref.shape[1], tile):
            value = qkv_ref[at // chunk, :, at % chunk : at % chunk + tile].astype(F32)
            j, inside = divmod(at, BLOCK)
            if inside < QW:
                to = j * QW + inside
            elif inside < QW + KW:
                to = PAIRS * QW + j * KW + inside - QW
            else:
                to = PAIRS * (QW + KW) + j * KW + inside - QW - KW
            qkv_grad_ref[:, to : to + tile] = value

    @pl.when(i == 4)
    def _():
        gain_one_ref[...] = few_ref[0:1]
        gain_two_ref[...] = few_ref[1:2]
        router_ref[...] = few_ref[8 : 8 + router_ref.shape[0]]


def unpack_weights(shares, out_total, qkv_total, few, hidden, out_home, input_grad, tall, short, experts):
    tokens, width = hidden.shape
    rows = out_total.shape[1]
    first, last = shares
    counts = (first.shape[0], last.shape[0], len(out_home))
    count = counts[0] + counts[1]
    step = tokens // 4
    block = pl.BlockSpec((step, width), lambda i: (jnp.minimum(i, 3), 0))
    splits = 4 if rows % 64 == 0 else 2
    short_rows = rows // splits
    one = (1,) + first.shape[1:]
    return pl.pallas_call(
        functools.partial(unpack_kernel, tall, short, counts),
        grid=(count,),
        in_specs=[
            pl.BlockSpec(one, lambda i: (jnp.minimum(i, counts[0] - 1), 0, 0)),
            pl.BlockSpec(one, lambda i: (jnp.maximum(i - counts[0], 0), 0, 0)),
        ]
        + [block] * (2 + len(out_home))
        + [
            pl.BlockSpec(
                (t.shape[0], short_rows, t.shape[2]), lambda i: (0, jnp.minimum(i, splits - 1), 0)
            )
            for t in (out_total, qkv_total)
        ]
        + [whole_spec(few.shape)],
        out_specs=[
            block,
            block,
            pl.BlockSpec((1, tall, 2 * FF), lambda i: (i, 0, 0)),
            pl.BlockSpec((1, short, width), lambda i: (i, 0, 0)),
            pl.BlockSpec((short_rows, HEADS * HEAD), lambda i: (jnp.minimum(i, splits - 1), 0)),
            pl.BlockSpec((short_rows, PAIRS * BLOCK), lambda i: (jnp.minimum(i, splits - 1), 0)),
            whole_spec((1, rows)),
            whole_spec((1, rows)),
            whole_spec((experts, rows)),
        ],
        out_shape=[
            jax.ShapeDtypeStruct(hidden.shape, BF16),
            jax.ShapeDtypeStruct(hidden.shape, F32),
            jax.ShapeDtypeStruct((count, tall, 2 * FF), F32),
            jax.ShapeDtypeStruct((count, short, width), F32),
            jax.ShapeDtypeStruct((rows, HEADS * HEAD), F32),
            jax.ShapeDtypeStruct((rows, PAIRS * BLOCK), F32),
            jax.ShapeDtypeStruct((1, rows), F32),
            jax.ShapeDtypeStruct((1, rows), F32),
            jax.ShapeDtypeStruct((experts, rows), F32),
        ],
        compiler_params=pltpu.CompilerParams(vmem_limit_bytes=62 << 20),
        cost_estimate=pl.CostEstimate(flops=10**7, bytes_accessed=24 << 20, transcendentals=0),
        name="unpack_weights",
    )(first, last, hidden, *out_home, input_grad, out_total, qkv_total, few)


def bands(count):
    return [(0, 2), (2, 3), (3, count)]


def local(
    inputs, attn_gain, qkv_weight, out_weight, ffn_gain, router_weight,
    expand_weight, project_weight, segment_ids, routes, out_grad,
):
    groups, shards = lax.axis_size("expert"), lax.axis_size("shard")
    tokens, width = inputs.shape
    experts = router_weight.shape[1]
    local_count = expand_weight.shape[0]
    capacity = 8 * ((5 * tokens * TOP + 32 * experts - 1) // (32 * experts))

    packed, *bands_packed = pack_weights(
        expand_weight, project_weight, qkv_weight, attn_gain, ffn_gain, router_weight
    )
    packed_full = [lax.all_gather(p, "shard", axis=0) for p in bands_packed]
    qkv_full, out_part, *u_others = gather_weights(
        [packed, out_weight], out_grad, groups, shards
    )
    qkv_full = qkv_full.reshape(width, -1)
    misc_rows = qkv_full[:, PAIRS * BLOCK :].T
    gain_one, gain_two = misc_rows[0:1], misc_rows[1:2]
    router_rows = misc_rows[8 : 8 + experts]
    tables = tuple(jnp.asarray(t) for t in rope_tables())
    seg_row = segment_ids.reshape(1, tokens)
    seg_col = segment_ids.reshape(tokens, 1)
    normed_t, proj, mixed, lse, out_full = attention_forward(
        inputs, gain_one, qkv_full, tables, seg_col, seg_row, out_part, groups, shards
    )
    hidden, ffn_in, gates, meta_own = middle(
        mixed, out_full, inputs, gain_two, router_rows, routes.T, groups
    )
    tall, short = expand_weight.shape[1], project_weight.shape[1]
    call = functools.partial(expert_call, capacity, shards, groups)

    cores = [[2 * z + core for z in range(shards // 2)] for core in range(2)]

    def share_out(dw):
        return lax.psum_scatter(
            dw, "shard", scatter_dimension=0, axis_index_groups=cores, tiled=True
        )[0]

    x_all, u_all, meta, out_acc, dx_acc, gg, dw = call(
        0, "first", (ffn_in, meta_own, out_grad, *u_others), packed_full[0]
    )
    shares = [share_out(dw)]
    out_acc, dx_acc, gg, dw = call(
        2, "between", (x_all, u_all, meta, out_acc, dx_acc, gg), packed_full[1]
    )
    *out_sent, dx_home, gg_home, dw = call(
        3, "last", (x_all, u_all, meta, out_acc, dx_acc, gg), packed_full[2], dw
    )
    shares.append(share_out(dw))
    sources = 3 if groups == 4 else groups
    hidden_grads, attended_grads, router_part, gain_two_grad = hidden_back(
        sources, dx_home, gg_home, gates, router_rows, hidden, gain_two, out_grad, ffn_in
    )
    dproj, out_sum = attention_backward(
        attended_grads, out_full, proj, mixed, lse, tables, seg_col, seg_row, groups, shards
    )
    out_total, qkv_total, few, input_grad, *out_came = reduce_weights(
        normed_t, dproj, gain_two_grad, router_part, out_sum, gain_one, qkv_full, inputs,
        hidden_grads, out_sent[1:], groups, shards,
    )
    output, input_grad, expand_grad, project_grad, out_weight_grad, qkv_grad, *gains = unpack_weights(
        shares, out_total, qkv_total, few, hidden, [out_sent[0], *out_came], input_grad, tall, short,
        experts,
    )
    return (
        output,
        input_grad,
        gains[0][0],
        qkv_grad,
        out_weight_grad,
        gains[1][0],
        gains[2].T,
        expand_grad,
        project_grad,
    )


def solution(mesh):
    rows = P(("expert", "shard"), None)
    return jax.shard_map(
        local,
        mesh=mesh,
        in_specs=(
            rows, P("shard"), P("shard", None), P("shard", None), P("shard"), P("shard", None),
            P("expert", "shard", None), P("expert", "shard", None), rows, rows, rows,
        ),
        out_specs=(
            rows, rows, P("shard"), P("shard", None), P("shard", None), P("shard"),
            P("shard", None), P("expert", "shard", None), P("expert", "shard", None),
        ),
        check_vma=False,
    )
```

profile of v0, /device:TPU:0, one launch (start us, length us, event | category | flops | bytes accessed | tf_op | source)
XLA Modules:
  0.0 535.3 jit_solution(5827197837307000934)
XLA Ops:
  7.2 0.0 all-gather.7.cloned.1.call-start
  7.2 4.1 pack_weights.1
  11.4 0.0 all-gather.9.cloned.1.call-start
  11.4 0.7 all-gather.9.cloned.1.call-update
  12.2 0.0 all-gather.11.cloned.1.call-start
  12.2 0.7 all-gather.11.cloned.1.call-update
  12.9 0.0 reduce-scatter.3.cloned.1.call-start
  12.9 0.9 copy.39.seg_col_ref
  13.8 78.1 %gather_weights.1 = (bf16[32,48,2688]{2,1,0:T(8,128)(2,1)}, bf16[32,48,1536]{2,1,0:T(8,128)(2,1)}, bf16[512,1536]{1,0:T(8,128)(2,1)}, bf16[512,1536]{1,0:T(8,128)(2,1)}) custom-call(bf16[4,48,2688]{2,1,0:T(8,128)(2,1)} %bitcast.22, bf16[4,48,1536]{2,1,0:T(8,128)(2,1)} %bitcast.23, bf16[512,1536]{1,0:T(8,128)(2,1)} %up_ref.1), custom_call_target="tpu_custom_call" | custom-call | tf_op jit(solution)/shard_map/gather_weights/pallas_call | solution.py:537
  91.9 1.0 slice_bitcast_fusion
  92.9 0.2 slice.19
  93.1 0.8 copy.41.router_ref
  93.9 0.2 fusion
  94.1 0.8 copy.40.gain_ref
  94.9 0.8 copy.38.gain_ref.refs_5_
  95.7 29.3 %attention_forward.1 = (bf16[1536,512]{1,0:T(8,128)(2,1)}, bf16[512,2560]{1,0:T(8,128)(2,1)}, bf16[512,1536]{1,0:T(8,128)(2,1)}, f32[4,512,8]{2,1,0:T(8,128)}, bf16[32,48,1536]{2,1,0:T(8,128)(2,1)}) custom-call(bf16[512,1536]{1,0:T(8,128)(2,1)} %refs_7_.1, bf16[1,1536]{1,0:T(2,128)(2,1)} %copy.38.gain_ref.refs_5_, ...), custom_call_target="tpu_custom_call", output_to_operand_aliasing={{4}: (8, {})} | custom-call | flops 10000000000 | bytes 20971520 | tf_op jit(solution)/shard_map/attention_forward/pallas_call | solution.py:150
  125.0 8.3 %middle.1 = (f32[512,1536]{1,0:T(8,128)}, bf16[512,1536]{1,0:T(8,128)(2,1)}, f32[20,512]{1,0:T(8,128)}, f32[4,16,512]{2,1,0:T(8,128)}) custom-call(bf16[512,1536]{1,0:T(8,128)(2,1)} %get-tuple-element.67.mixed_ref.all_ref, bf16[1536,1536]{1,0:T(8,128)(2,1)} %bitcast.29, bf16[512,1536]{1,0:T(8,128)(2,1)} %refs_7_.1, bf16[1,1536]{1,0:T(2,128)(2,1)} %copy.40.gain_ref, ...), custom_call_target="tpu_custom_call" | custom-call | flops 3000000000 | bytes 16777216 | tf_op jit(solution)/shard_map/middle/pallas_call | solution.py:330
  133.2 0.1 all-gather.7.cloned.1.call-done
  133.3 107.9 %experts_first.1 = (bf16[4,512,1536]{2,1,0:T(8,128)(2,1)}, bf16[4,512,1536]{2,1,0:T(8,128)(2,1)}, f32[4,16,512]{2,1,0:T(8,128)}, bf16[4,512,1536]{2,1,0:T(8,128)...) custom-call(bf16[512,1536]{1,0:T(8,128)(2,1)} %get-tuple-element.69.refs_0_.ffn_ref, ...), custom_call_target="tpu_custom_call" | custom-call | flops 41875931136 | bytes 37748736 | tf_op jit(solution)/shard_map/experts_first/pallas_call | solution.py:1424
  241.2 0.0 reduce-scatter.3.cloned.1.call-update
  241.2 0.0 reduce-scatter.5.cloned.1.call-start
  241.3 0.0 all-gather.9.cloned.1.call-done
  241.3 34.9 %experts_between.1 = (bf16[4,512,1536]{2,1,0:T(8,128)(2,1)}, bf16[4,512,1536]{2,1,0:T(8,128)(2,1)}, f32[4,8,512]{2,1,0:T(8,128)}, bf16[4,2,288,1024]{3,2,1,0:T(8,128)(2,1)}) custom-call(bf16[4,512,1536]{2,1,0:T(8,128)(2,1)} %get-tuple-element.75.refs_0_, bf16[4,512,1536]{2,1,0:T(8,128)(2,1)} %get-tuple-element.76.refs_1_, ...), custom_call_target="tpu_custom_call" | custom-call | flops 20937965568 | bytes 37748736 | tf_op jit(solution)/shard_map/experts_between/pallas_call | solution.py:1424
  276.2 2.0 all-gather.11.cloned.1.call-done
  278.2 87.4 %experts_last.1 = (bf16[512,1536]{1,0:T(8,128)(2,1)}, bf16[512,1536]{1,0:T(8,128)(2,1)}, bf16[512,1536]{1,0:T(8,128)(2,1)}, bf16[4,512,1536]{2,1,0:T(8,128)(2,1)...) custom-call(bf16[4,512,1536]{2,1,0:T(8,128)(2,1)} %get-tuple-element.75.refs_0_, ...), custom_call_target="tpu_custom_call" | custom-call | flops 41875931136 | bytes 37748736 | tf_op jit(solution)/shard_map/experts_last/pallas_call | solution.py:1424
  365.6 0.0 reduce-scatter.5.cloned.1.call-update
  365.7 7.9 %hidden_back.1 = (f32[512,1536]{1,0:T(8,128)}, bf16[512,1536]{1,0:T(8,128)(2,1)}, f32[20,1536]{1,0:T(8,128)}, f32[1,1536]{1,0:T(1,128)}) custom-call(bf16[4,512,1536]{2,1,0:T(8,128)(2,1)} %get-tuple-element.91.dx_ref, f32[4,8,512]{2,1,0:T(8,128)} %get-tuple-element.92.gg_ref, f32[20,512]{1,0:T(8,128)} %get-tuple-element.93.gates_ref, ...), custom_call_target="tpu_custom_call" | custom-call | flops 100000000 | bytes 20971520 | tf_op jit(solution)/shard_map/hidden_back/pallas_call | solution.py:1529
  373.6 39.1 %attention_backward.1 = (bf16[512,2560]{1,0:T(8,128)(2,1)}, bf16[4,192,384]{2,1,0:T(8,128)(2,1)}) custom-call(bf16[512,1536]{1,0:T(8,128)(2,1)} %get-tuple-element.94.ag_ref, bf16[1536,1536]{1,0:T(8,128)(2,1)} %bitcast.30, bf16[512,2560]{1,0:T(8,128)(2,1)} %get-tuple-element.95.proj_ref, bf16[512,1536]{1,0:T(8,128)(2,1)} %get-tuple-element.67.mixed_ref.all_ref, ...), custom_call_target="tpu_custom_call" | custom-call | flops 10000000000 | bytes 20971520 | tf_op jit(solution)/shard_map/attention_backward/pallas_call | solution.py:262
  412.7 105.2 %reduce_weights.1 = (bf16[4,192,384]{2,1,0:T(8,128)(2,1)}, bf16[4,192,640]{2,1,0:T(8,128)(2,1)}, f32[32,192]{1,0:T(8,128)}, f32[512,1536]{1,0:T(8,128)}, bf16[51...) custom-call(bf16[1536,512]{1,0:T(8,128)(2,1)} %get-tuple-element.90.refs_0_, bf16[512,2560]{1,0:T(8,128)(2,1)} %get-tuple-element.97.refs_1_, ...), custom_call_target="tpu_custom_call" | custom-call | flops 4026531840 | bytes 8388608 | tf_op jit(solution)/shard_map/reduce_weights/pallas_call | solution.py:893
  518.0 0.0 reduce-scatter.3.cloned.1.call-done
  518.0 0.0 reduce-scatter.5.cloned.1.call-done
  518.0 10.5 %unpack_weights.1 = (bf16[512,1536]{1,0:T(8,128)(2,1)}, f32[512,1536]{1,0:T(8,128)}, f32[5,192,1024]{2,1,0:T(8,128)}, f32[5,64,1536]{2,1,0:T(8,128)}, f32[192,15...) custom-call(bf16[2,288,1024]{2,1,0:T(8,128)(2,1)} %bitcast.21, ...), custom_call_target="tpu_custom_call" | custom-call | flops 10000000 | bytes 25165824 | tf_op jit(solution)/shard_map/unpack_weights/pallas_call | solution.py:1625
  (3 shorter events, 0.0 us)
Async XLA Ops:
  7.2 126.1 %all-gather.7.cloned.1.call-start = ((), (), s32[]{:S(2)}) async-start(), calls=%async_computation.4 | async-start | bytes 10616832 | tf_op jit(solution)/shard_map/all_gather | solution.py:1685
  7.2 5.7 %copy-start = (s32[1,512]{1,0:T(1,128)S(1)}, s32[1,512]{1,0:T(1,128)}, u32[]{:S(2)}) copy-start(s32[1,512]{1,0:T(1,128)} %seg_row_ref.3) | copy-start | bytes 6148
  11.4 229.9 %all-gather.9.cloned.1.call-start = ((), (), s32[]{:S(2)}) async-start(), calls=%async_computation.5 | async-start | bytes 5308416 | tf_op jit(solution)/shard_map/all_gather | solution.py:1685
  12.2 266.0 %all-gather.11.cloned.1.call-start = ((), (), s32[]{:S(2)}) async-start(), calls=%async_computation.6 | async-start | bytes 10616832 | tf_op jit(solution)/shard_map/all_gather | solution.py:1685
  12.9 505.1 %reduce-scatter.3.cloned.1.call-start = ((), (), s32[]{:S(2)}) async-start(), calls=%async_computation.2 | async-start | bytes 5898240 | tf_op jit(solution)/shard_map/reduce_scatter | solution.py:1708
  241.2 276.8 %reduce-scatter.5.cloned.1.call-start = ((), (), s32[]{:S(2)}) async-start(), calls=%async_computation.3 | async-start | bytes 8847360 | tf_op jit(solution)/shard_map/reduce_scatter | solution.py:1708
Sparse Core Ops, SparseCore 0:
  11.5 121.7 all-gather.6
  135.5 50.8 all-gather.8
  188.6 89.5 all-gather.10
  280.3 83.6 reduce-scatter.2
  366.2 150.3 reduce-scatter.4
where the time goes:
time: 543 us; the launch traced here: 535 us
  Pallas kernels  513 us (94%)
  between operations  14.1 us (3%)
    pallas_call x3, Pallas kernels, expert_call(): pl.pallas_call(functools.partial(expert_kernel, capacity, shards, groups,...  230 us
    pallas_call x1, Pallas kernels, reduce_weights(): pl.pallas_call(functools.partial(reduce_kernel, groups, levels), in_specs...  105 us
    pallas_call x1, Pallas kernels, gather_weights(): pl.pallas_call(functools.partial(gather_kernel, groups, parts, levels), i...  78.1 us
    pallas_call x1, Pallas kernels, attention_backward(): pl.pallas_call(functools.partial(attention_backward_kernel, groups, level...  39.1 us
    pallas_call x1, Pallas kernels, attention_forward(): pl.pallas_call(functools.partial(attention_forward_kernel, parts, levels)...  29.3 us
  transfers between devices with their start and end apart: 5, of which 2 were waited for; matrix products, arithmetic and copies ran while one was open for 1% of the time, Pallas kernels for 93%

commit v1 on v0

--- a/solution.py
+++ b/solution.py
@@ -1524,7 +1524,7 @@
 def hidden_back(sources, dx_home, gg_home, gates, router_rows, hidden, gain_row, out_grad, ffn_in):
     groups, tokens, width = dx_home.shape
     experts = gates.shape[0]
-    step = 128
+    step = 256
     rows = pl.BlockSpec((step, width), lambda i: (i, 0))
     return pl.pallas_call(
         hidden_back_kernel,

time: 543 us -> 543 us (level)
  no operation moved by 1% of the time
where the time goes in v1:
time: 543 us; the launch traced here: 536 us
  Pallas kernels  513 us (94%)
  between operations  14.1 us (3%)
    pallas_call x3, Pallas kernels, expert_call(): pl.pallas_call(functools.partial(expert_kernel, capacity, shards, groups,...  230 us
    pallas_call x1, Pallas kernels, reduce_weights(): pl.pallas_call(functools.partial(reduce_kernel, groups, levels), in_specs...  106 us
    pallas_call x1, Pallas kernels, gather_weights(): pl.pallas_call(functools.partial(gather_kernel, groups, parts, levels), i...  78.1 us
    pallas_call x1, Pallas kernels, attention_backward(): pl.pallas_call(functools.partial(attention_backward_kernel, groups, level...  39.6 us
    pallas_call x1, Pallas kernels, attention_forward(): pl.pallas_call(functools.partial(attention_forward_kernel, parts, levels)...  29.3 us
  transfers between devices with their start and end apart: 5, of which 2 were waited for; matrix products, arithmetic and copies ran while one was open for 1% of the time, Pallas kernels for 93%

profile of v1, /device:TPU:0, one launch (start us, length us, event | category | flops | bytes accessed | tf_op | source)
XLA Modules:
  0.0 535.5 jit_solution(5674530514595342433)
XLA Ops:
  7.2 0.0 all-gather.7.cloned.1.call-start
  7.2 4.1 pack_weights.1
  11.4 0.0 all-gather.9.cloned.1.call-start
  11.4 0.7 all-gather.9.cloned.1.call-update
  12.2 0.0 all-gather.11.cloned.1.call-start
  12.2 0.7 all-gather.11.cloned.1.call-update
  12.9 0.0 reduce-scatter.3.cloned.1.call-start
  12.9 0.9 copy.39.seg_col_ref
  13.8 78.1 %gather_weights.1 = (bf16[32,48,2688]{2,1,0:T(8,128)(2,1)}, bf16[32,48,1536]{2,1,0:T(8,128)(2,1)}, bf16[512,1536]{1,0:T(8,128)(2,1)}, bf16[512,1536]{1,0:T(8,128)(2,1)}) custom-call(bf16[4,48,2688]{2,1,0:T(8,128)(2,1)} %bitcast.22, bf16[4,48,1536]{2,1,0:T(8,128)(2,1)} %bitcast.23, bf16[512,1536]{1,0:T(8,128)(2,1)} %up_ref.1), custom_call_target="tpu_custom_call" | custom-call | tf_op jit(solution)/shard_map/gather_weights/pallas_call | solution.py:537
  91.9 1.0 slice_bitcast_fusion
  92.9 0.2 slice.19
  93.1 0.8 copy.41.router_ref
  93.9 0.2 fusion
  94.1 0.8 copy.40.gain_ref
  94.9 0.8 copy.38.gain_ref.refs_5_
  95.7 29.3 %attention_forward.1 = (bf16[1536,512]{1,0:T(8,128)(2,1)}, bf16[512,2560]{1,0:T(8,128)(2,1)}, bf16[512,1536]{1,0:T(8,128)(2,1)}, f32[4,512,8]{2,1,0:T(8,128)}, bf16[32,48,1536]{2,1,0:T(8,128)(2,1)}) custom-call(bf16[512,1536]{1,0:T(8,128)(2,1)} %refs_7_.1, bf16[1,1536]{1,0:T(2,128)(2,1)} %copy.38.gain_ref.refs_5_, ...), custom_call_target="tpu_custom_call", output_to_operand_aliasing={{4}: (8, {})} | custom-call | flops 10000000000 | bytes 20971520 | tf_op jit(solution)/shard_map/attention_forward/pallas_call | solution.py:150
  125.0 8.3 %middle.1 = (f32[512,1536]{1,0:T(8,128)}, bf16[512,1536]{1,0:T(8,128)(2,1)}, f32[20,512]{1,0:T(8,128)}, f32[4,16,512]{2,1,0:T(8,128)}) custom-call(bf16[512,1536]{1,0:T(8,128)(2,1)} %get-tuple-element.67.mixed_ref.all_ref, bf16[1536,1536]{1,0:T(8,128)(2,1)} %bitcast.29, bf16[512,1536]{1,0:T(8,128)(2,1)} %refs_7_.1, bf16[1,1536]{1,0:T(2,128)(2,1)} %copy.40.gain_ref, ...), custom_call_target="tpu_custom_call" | custom-call | flops 3000000000 | bytes 16777216 | tf_op jit(solution)/shard_map/middle/pallas_call | solution.py:330
  133.2 0.1 all-gather.7.cloned.1.call-done
  133.3 107.9 %experts_first.1 = (bf16[4,512,1536]{2,1,0:T(8,128)(2,1)}, bf16[4,512,1536]{2,1,0:T(8,128)(2,1)}, f32[4,16,512]{2,1,0:T(8,128)}, bf16[4,512,1536]{2,1,0:T(8,128)...) custom-call(bf16[512,1536]{1,0:T(8,128)(2,1)} %get-tuple-element.69.refs_0_.ffn_ref, ...), custom_call_target="tpu_custom_call" | custom-call | flops 41875931136 | bytes 37748736 | tf_op jit(solution)/shard_map/experts_first/pallas_call | solution.py:1424
  241.2 0.0 reduce-scatter.3.cloned.1.call-update
  241.2 0.0 reduce-scatter.5.cloned.1.call-start
  241.3 0.0 all-gather.9.cloned.1.call-done
  241.3 34.9 %experts_between.1 = (bf16[4,512,1536]{2,1,0:T(8,128)(2,1)}, bf16[4,512,1536]{2,1,0:T(8,128)(2,1)}, f32[4,8,512]{2,1,0:T(8,128)}, bf16[4,2,288,1024]{3,2,1,0:T(8,128)(2,1)}) custom-call(bf16[4,512,1536]{2,1,0:T(8,128)(2,1)} %get-tuple-element.75.refs_0_, bf16[4,512,1536]{2,1,0:T(8,128)(2,1)} %get-tuple-element.76.refs_1_, ...), custom_call_target="tpu_custom_call" | custom-call | flops 20937965568 | bytes 37748736 | tf_op jit(solution)/shard_map/experts_between/pallas_call | solution.py:1424
  276.2 2.0 all-gather.11.cloned.1.call-done
  278.2 87.4 %experts_last.1 = (bf16[512,1536]{1,0:T(8,128)(2,1)}, bf16[512,1536]{1,0:T(8,128)(2,1)}, bf16[512,1536]{1,0:T(8,128)(2,1)}, bf16[4,512,1536]{2,1,0:T(8,128)(2,1)...) custom-call(bf16[4,512,1536]{2,1,0:T(8,128)(2,1)} %get-tuple-element.75.refs_0_, ...), custom_call_target="tpu_custom_call" | custom-call | flops 41875931136 | bytes 37748736 | tf_op jit(solution)/shard_map/experts_last/pallas_call | solution.py:1424
  365.6 0.0 reduce-scatter.5.cloned.1.call-update
  365.7 7.0 %hidden_back.1 = (f32[512,1536]{1,0:T(8,128)}, bf16[512,1536]{1,0:T(8,128)(2,1)}, f32[20,1536]{1,0:T(8,128)}, f32[1,1536]{1,0:T(1,128)}) custom-call(bf16[4,512,1536]{2,1,0:T(8,128)(2,1)} %get-tuple-element.91.dx_ref, f32[4,8,512]{2,1,0:T(8,128)} %get-tuple-element.92.gg_ref, f32[20,512]{1,0:T(8,128)} %get-tuple-element.93.gates_ref, ...), custom_call_target="tpu_custom_call" | custom-call | flops 100000000 | bytes 20971520 | tf_op jit(solution)/shard_map/hidden_back/pallas_call | solution.py:1529
  372.6 39.6 %attention_backward.1 = (bf16[512,2560]{1,0:T(8,128)(2,1)}, bf16[4,192,384]{2,1,0:T(8,128)(2,1)}) custom-call(bf16[512,1536]{1,0:T(8,128)(2,1)} %get-tuple-element.94.ag_ref, bf16[1536,1536]{1,0:T(8,128)(2,1)} %bitcast.30, bf16[512,2560]{1,0:T(8,128)(2,1)} %get-tuple-element.95.proj_ref, bf16[512,1536]{1,0:T(8,128)(2,1)} %get-tuple-element.67.mixed_ref.all_ref, ...), custom_call_target="tpu_custom_call" | custom-call | flops 10000000000 | bytes 20971520 | tf_op jit(solution)/shard_map/attention_backward/pallas_call | solution.py:262
  412.3 105.9 %reduce_weights.1 = (bf16[4,192,384]{2,1,0:T(8,128)(2,1)}, bf16[4,192,640]{2,1,0:T(8,128)(2,1)}, f32[32,192]{1,0:T(8,128)}, f32[512,1536]{1,0:T(8,128)}, bf16[51...) custom-call(bf16[1536,512]{1,0:T(8,128)(2,1)} %get-tuple-element.90.refs_0_, bf16[512,2560]{1,0:T(8,128)(2,1)} %get-tuple-element.97.refs_1_, ...), custom_call_target="tpu_custom_call" | custom-call | flops 4026531840 | bytes 8388608 | tf_op jit(solution)/shard_map/reduce_weights/pallas_call | solution.py:893
  518.2 0.0 reduce-scatter.3.cloned.1.call-done
  518.2 0.0 reduce-scatter.5.cloned.1.call-done
  518.2 10.5 %unpack_weights.1 = (bf16[512,1536]{1,0:T(8,128)(2,1)}, f32[512,1536]{1,0:T(8,128)}, f32[5,192,1024]{2,1,0:T(8,128)}, f32[5,64,1536]{2,1,0:T(8,128)}, f32[192,15...) custom-call(bf16[2,288,1024]{2,1,0:T(8,128)(2,1)} %bitcast.21, ...), custom_call_target="tpu_custom_call" | custom-call | flops 10000000 | bytes 25165824 | tf_op jit(solution)/shard_map/unpack_weights/pallas_call | solution.py:1625
  (3 shorter events, 0.0 us)
Async XLA Ops:
  7.2 126.1 %all-gather.7.cloned.1.call-start = ((), (), s32[]{:S(2)}) async-start(), calls=%async_computation.4 | async-start | bytes 10616832 | tf_op jit(solution)/shard_map/all_gather | solution.py:1685
  7.2 5.7 %copy-start = (s32[1,512]{1,0:T(1,128)S(1)}, s32[1,512]{1,0:T(1,128)}, u32[]{:S(2)}) copy-start(s32[1,512]{1,0:T(1,128)} %seg_row_ref.3) | copy-start | bytes 6148
  11.4 229.9 %all-gather.9.cloned.1.call-start = ((), (), s32[]{:S(2)}) async-start(), calls=%async_computation.5 | async-start | bytes 5308416 | tf_op jit(solution)/shard_map/all_gather | solution.py:1685
  12.2 266.0 %all-gather.11.cloned.1.call-start = ((), (), s32[]{:S(2)}) async-start(), calls=%async_computation.6 | async-start | bytes 10616832 | tf_op jit(solution)/shard_map/all_gather | solution.py:1685
  12.9 505.3 %reduce-scatter.3.cloned.1.call-start = ((), (), s32[]{:S(2)}) async-start(), calls=%async_computation.2 | async-start | bytes 5898240 | tf_op jit(solution)/shard_map/reduce_scatter | solution.py:1708
  241.2 277.0 %reduce-scatter.5.cloned.1.call-start = ((), (), s32[]{:S(2)}) async-start(), calls=%async_computation.3 | async-start | bytes 8847360 | tf_op jit(solution)/shard_map/reduce_scatter | solution.py:1708
Sparse Core Ops, SparseCore 0:
  11.5 121.7 all-gather.6
  135.5 50.8 all-gather.8
  188.6 89.5 all-gather.10
  280.3 83.6 reduce-scatter.2
  366.2 150.3 reduce-scatter.4
